TPU v7x, 32 devices: a whole 2x2x4 slice. The times are simulated.
32 devices in a mesh: batch: 8 (over z, x), head: 4 (over y, core).
Axes of the slice: x: 2, y: 2, z: 4, core: 2. Of those that a mesh axis runs over, the one named last changes fastest.
Arguments:
- block_input: bfloat16 [64, 1024, 768], P(('batch', 'head')), may hold values from -6 to 6
- cotangent: bfloat16 [64, 1024, 768], P(('batch', 'head')), may hold values from -6 to 6
- segment_lengths: int32 [64, 8], P('batch'), may hold values from 1 to 256, 1024 in all within a row
- thought_counts: int32 [64, 8], P('batch'), may hold values from 0 to 3
- packing_mask: int32 [64, 1024], P(('batch', 'head')), may hold values 0 or 1
- attend_weight: float32 [768, 3, 768], P('batch', None, 'head')
- output_weight: float32 [768, 768], P(('batch', 'head'))
- expand_weight: float32 [768, 3072], P(('batch', 'head'))
- reduce_weight: float32 [3072, 768], P(('batch', 'head'))
- vectors: float32 [768, 12], P(('batch', 'head'))
- first_attend: float32 [768, 3, 768], P('batch', None, 'head')
- first_output: float32 [768, 768], P(('batch', 'head'))
- first_expand: float32 [768, 3072], P(('batch', 'head'))
- first_reduce: float32 [3072, 768], P(('batch', 'head'))
- first_vectors: float32 [768, 12], P(('batch', 'head'))
- second_attend: float32 [768, 3, 768], P('batch', None, 'head'), as said below
- second_output: float32 [768, 768], P(('batch', 'head')), as said below
- second_expand: float32 [768, 3072], P(('batch', 'head')), as said below
- second_reduce: float32 [3072, 768], P(('batch', 'head')), as said below
- second_vectors: float32 [768, 12], P(('batch', 'head')), as said below
Outputs:
- hidden_states: bfloat16 [64, 1024, 768], P(('batch', 'head'))
- input_gradient: bfloat16 [64, 1024, 768], P(('batch', 'head'))
- moment_attend: float32 [768, 3, 768], P('batch', None, 'head')
- moment_output: float32 [768, 768], P(('batch', 'head'))
- moment_expand: float32 [768, 3072], P(('batch', 'head'))
- moment_reduce: float32 [3072, 768], P(('batch', 'head'))
- moment_vectors: float32 [768, 12], P(('batch', 'head'))
- square_attend: float32 [768, 3, 768], P('batch', None, 'head')
- square_output: float32 [768, 768], P(('batch', 'head'))
- square_expand: float32 [768, 3072], P(('batch', 'head'))
- square_reduce: float32 [3072, 768], P(('batch', 'head'))
- square_vectors: float32 [768, 12], P(('batch', 'head'))
- master_attend: float32 [768, 3, 768], P('batch', None, 'head')
- master_output: float32 [768, 768], P(('batch', 'head'))
- master_expand: float32 [768, 3072], P(('batch', 'head'))
- master_reduce: float32 [3072, 768], P(('batch', 'head'))
- master_vectors: float32 [768, 12], P(('batch', 'head'))
- trust_norms: float32 [3, 16], replicated
Inputs may be any that keep to these rules, and one draw needn't show every extreme that they name: `segment_lengths`: each row's lengths sum to 1024. `second_attend`: positive. `second_output`: positive. `second_expand`: positive. `second_reduce`: positive. `second_vectors`: positive.
All inputs are finite; a program needn't handle non-finite values. No bound on the sum of `packing_mask` on one device may be relied on, other than what follows from the above.
Results may differ from a plain program's by a relative error of at most 0.013.
The roundings to bfloat16 on the way count: a program that leaves them out, or rounds other values in their place, can miss the bound.
Values may be sent and summed in bfloat16 or wider, within the bound.
No kernel may reach another device: no remote copies, remote signals or barrier semaphores. Data moves between devices by JAX's collectives and lax.ppermute only.
A program may use at most 256 MiB of HBM per device.

v0:
```python
import jax
import jax.numpy as jnp
from jax import lax
from jax.sharding import PartitionSpec as P

HEAD_DIM = 64
MICRO = 2
THOUGHT_TOKENS = 8
STEP = 6


NORM_EPS = 1e-05
NEGATIVE = -1e30
BETA = 0.5
RATE = 0.5
DECAY = 0.01
ADAM_EPS = 1e-06


def layer_norm(values, gain, shift):
    centre = values - jnp.mean(values, axis=-1, keepdims=True)
    factor = lax.rsqrt(jnp.mean(centre * centre, axis=-1, keepdims=True) + NORM_EPS)
    normed = centre * factor
    return (normed * gain + shift, normed, factor)


def norm_back(grad, normed, factor, gain):
    inner = grad * gain
    return factor * (
        inner
        - jnp.mean(inner, axis=-1, keepdims=True)
        - normed * jnp.mean(inner * normed, axis=-1, keepdims=True)
    )


def gelu_tanh(values):
    return jax.nn.gelu(values, approximate=True)


def segment_ids(lengths, positions):
    ends = jnp.cumsum(lengths, axis=-1)
    return jnp.sum((positions[None, :, None] >= ends[:, None, :]).astype(jnp.int32), axis=-1)


def loss_weight(lengths, counts, mask, span):
    positions = jnp.arange(span, dtype=jnp.int32)
    ends = jnp.cumsum(lengths, axis=-1)
    starts = ends - lengths
    segment = segment_ids(lengths, positions)
    onehot = segment[:, :, None] == jnp.arange(lengths.shape[-1], dtype=jnp.int32)[None, None, :]
    start_of = jnp.sum(jnp.where(onehot, starts[:, None, :], 0), axis=-1)
    passes = jnp.sum(jnp.where(onehot, counts[:, None, :], 0), axis=-1)
    keep = (positions[None, :] - start_of >= THOUGHT_TOKENS * passes) & (mask > 0)
    return keep.astype(jnp.float32)


def block_scores(query_block, key_rows, segment, start, block):
    length = key_rows.shape[0]
    scale = query_block.shape[2] ** (-0.5)
    key_place = jnp.arange(length, dtype=jnp.int32)
    query_place = start + jnp.arange(block, dtype=jnp.int32)
    query_segment = lax.dynamic_slice_in_dim(segment, start, block, 0)
    allowed = (key_place[None, :] <= query_place[:, None]) & (
        segment[None, :] == query_segment[:, None]
    )
    scores = (
        jnp.einsum("qhd,khd->hqk", query_block, key_rows, preferred_element_type=jnp.float32)
        * scale
    )
    return jnp.where(allowed[None], scores, NEGATIVE)


def attend_forward(query, key_rows, value_rows, segment):
    length, heads, width = query.shape
    block = min(512, length)

    def one_block(number):
        start = number * block
        query_block = lax.dynamic_slice_in_dim(query, start, block, 0)
        scores = block_scores(query_block, key_rows, segment, start, block)
        top = jnp.max(scores, axis=-1, keepdims=True)
        logsum = top + jnp.log(jnp.sum(jnp.exp(scores - top), axis=-1, keepdims=True))
        probs = jnp.exp(scores - logsum).astype(jnp.bfloat16)
        result = jnp.einsum("hqk,khd->qhd", probs, value_rows, preferred_element_type=jnp.float32)
        return (result, logsum[..., 0])

    results, logsums = lax.map(one_block, jnp.arange(length // block))
    return (results.reshape(length, heads, width), logsums)


def attend_backward(query, key_rows, value_rows, segment, logsums, grad_rows):
    length, heads, width = query.shape
    block = min(512, length)
    scale = width ** (-0.5)

    def one_block(carry, number):
        grad_key, grad_value = carry
        start = number * block
        query_block = lax.dynamic_slice_in_dim(query, start, block, 0)
        grad_block = lax.dynamic_slice_in_dim(grad_rows, start, block, 0)
        scores = block_scores(query_block, key_rows, segment, start, block)
        probs = jnp.exp(scores - logsums[number][..., None])
        low_probs = probs.astype(jnp.bfloat16)
        grad_value = grad_value + jnp.einsum(
            "hqk,qhd->khd", low_probs, grad_block, preferred_element_type=jnp.float32
        )
        grad_probs = jnp.einsum(
            "qhd,khd->hqk", grad_block, value_rows, preferred_element_type=jnp.float32
        )
        inner = jnp.sum(grad_probs * probs, axis=-1, keepdims=True)
        grad_scores = (probs * (grad_probs - inner)).astype(jnp.bfloat16)
        grad_query = (
            jnp.einsum("hqk,khd->qhd", grad_scores, key_rows, preferred_element_type=jnp.float32)
            * scale
        )
        grad_key = (
            grad_key
            + jnp.einsum(
                "hqk,qhd->khd", grad_scores, query_block, preferred_element_type=jnp.float32
            )
            * scale
        )
        return ((grad_key, grad_value), grad_query)

    empty = jnp.zeros((length, heads, width), jnp.float32)
    (grad_key, grad_value), grad_queries = lax.scan(
        one_block, (empty, empty), jnp.arange(length // block)
    )
    return (grad_queries.reshape(length, heads, width), grad_key, grad_value)


def fetch(attend_weight, output_weight, expand_weight, reduce_weight, vectors):
    attend_complete = lax.all_gather(
        attend_weight.astype(jnp.bfloat16), "batch", axis=0, tiled=True
    )
    shared = (
        lax.all_gather(output_weight.astype(jnp.bfloat16), ("batch", "head"), axis=0, tiled=True),
        lax.all_gather(expand_weight.astype(jnp.bfloat16), ("batch", "head"), axis=0, tiled=True),
        lax.all_gather(reduce_weight.astype(jnp.bfloat16), ("batch", "head"), axis=0, tiled=True),
        lax.all_gather(vectors.astype(jnp.bfloat16), ("batch", "head"), axis=0, tiled=True),
    )
    return (attend_complete, shared)


def adapt(grad, first, second, weight):
    moment = BETA * first + (1.0 - BETA) * grad
    square = BETA * second + (1.0 - BETA) * grad * grad
    correct = 1.0 - BETA**STEP
    update = moment / correct / (jnp.sqrt(square / correct) + ADAM_EPS) + DECAY * weight
    return (moment, square, update)


def shards(
    block_input,
    cotangent,
    segment_lengths,
    thought_counts,
    packing_mask,
    attend_weight,
    output_weight,
    expand_weight,
    reduce_weight,
    vectors,
    first_attend,
    first_output,
    first_expand,
    first_reduce,
    first_vectors,
    second_attend,
    second_output,
    second_expand,
    second_reduce,
    second_vectors,
):
    head_count = lax.axis_size("head")
    head_place = lax.axis_index("head")
    rows_here = block_input.shape[0]
    length = block_input.shape[1]
    model = block_input.shape[2]
    hidden_width = expand_weight.shape[1]
    seqs = rows_here // MICRO
    segs = segment_lengths.shape[1]
    positions = jnp.arange(length, dtype=jnp.int32)
    own_lengths = lax.dynamic_slice_in_dim(segment_lengths, head_place * rows_here, rows_here, 0)
    own_counts = lax.dynamic_slice_in_dim(thought_counts, head_place * rows_here, rows_here, 0)
    grouped_lengths = segment_lengths.reshape(head_count, rows_here, segs)
    total_attend = None
    total_output = jnp.zeros((model, model), jnp.float32)
    total_expand = jnp.zeros((model, hidden_width), jnp.float32)
    total_reduce = jnp.zeros((hidden_width, model), jnp.float32)
    total_vectors = jnp.zeros((model, vectors.shape[1]), jnp.float32)
    hidden_parts = []
    input_parts = []
    for micro_index in range(MICRO):
        lower = micro_index * seqs
        upper = lower + seqs
        current = fetch(attend_weight, output_weight, expand_weight, reduce_weight, vectors)
        attend_complete, shared = current
        output_complete, expand_complete, reduce_complete, vectors_low = shared
        model_parameters = vectors_low.astype(jnp.float32)
        width = attend_complete.shape[2]
        heads_here = width // HEAD_DIM
        rows = block_input[lower:upper].astype(jnp.float32)
        normed_out, normed_first, factor_first = layer_norm(
            rows, model_parameters[:, 0], model_parameters[:, 1]
        )
        normed_low = normed_out.astype(jnp.bfloat16)
        complete_normed = lax.all_gather(normed_low, "head", axis=0, tiled=True)
        group_lengths = grouped_lengths[:, lower:upper].reshape(head_count * seqs, segs)
        query_bias = lax.dynamic_slice_in_dim(model_parameters[:, 2], head_place * width, width, 0)
        value_bias = lax.dynamic_slice_in_dim(model_parameters[:, 3], head_place * width, width, 0)
        count = complete_normed.shape[0]
        shaped = (count, length, heads_here, HEAD_DIM)
        segment = segment_ids(group_lengths, positions)
        project_layer = jnp.einsum(
            "jie,eym->jiym", complete_normed, attend_complete, preferred_element_type=jnp.float32
        )
        query = (project_layer[:, :, 0] + query_bias).astype(jnp.bfloat16).reshape(shaped)
        key_rows = project_layer[:, :, 1].astype(jnp.bfloat16).reshape(shaped)
        value_rows = (project_layer[:, :, 2] + value_bias).astype(jnp.bfloat16).reshape(shaped)
        attended, logsums = lax.map(
            lambda parts: attend_forward(*parts), (query, key_rows, value_rows, segment)
        )
        heads_out = attended.reshape(count, length, width).astype(jnp.bfloat16)
        context_rows = lax.all_to_all(heads_out, "head", split_axis=0, concat_axis=2, tiled=True)
        middle = (
            rows
            + jnp.einsum(
                "gxp,ph->gxh", context_rows, output_complete, preferred_element_type=jnp.float32
            )
            + model_parameters[:, 4]
        )
        second_out, normed_second, factor_second = layer_norm(
            middle, model_parameters[:, 5], model_parameters[:, 6]
        )
        middle_normed = second_out.astype(jnp.bfloat16)
        preactivation = jnp.einsum(
            "nwj,jp->nwp", middle_normed, expand_complete, preferred_element_type=jnp.float32
        ) + model_parameters[:, 8:].T.reshape(-1)
        hidden_activated = gelu_tanh(preactivation).astype(jnp.bfloat16)
        result = (
            middle
            + jnp.einsum(
                "tkx,xw->tkw", hidden_activated, reduce_complete, preferred_element_type=jnp.float32
            )
            + model_parameters[:, 7]
        )
        hidden_parts.append(result.astype(jnp.bfloat16))
        current = fetch(attend_weight, output_weight, expand_weight, reduce_weight, vectors)
        attend_reverse, shared_back = current
        output_reverse, expand_reverse, reduce_reverse, vectors_back = shared_back
        weight_rows = loss_weight(
            own_lengths[lower:upper], own_counts[lower:upper], packing_mask[lower:upper], length
        )
        grad_out = cotangent[lower:upper].astype(jnp.float32) * weight_rows[..., None]
        branch_gradient = grad_out.astype(jnp.bfloat16)
        total_reduce = total_reduce + jnp.einsum(
            "qth,qtu->hu", hidden_activated, branch_gradient, preferred_element_type=jnp.float32
        )
        grad_act = jnp.einsum(
            "xzu,bu->xzb", branch_gradient, reduce_reverse, preferred_element_type=jnp.float32
        )
        unused, pull = jax.vjp(gelu_tanh, preactivation)
        preactivation_gradient = pull(grad_act)[0].astype(jnp.bfloat16)
        total_expand = total_expand + jnp.einsum(
            "eon,eoc->nc", middle_normed, preactivation_gradient, preferred_element_type=jnp.float32
        )
        grad_normed_mid = jnp.einsum(
            "xnm,pm->xnp",
            preactivation_gradient,
            expand_reverse,
            preferred_element_type=jnp.float32,
        )
        grad_middle = grad_out + norm_back(
            grad_normed_mid, normed_second, factor_second, model_parameters[:, 5]
        )
        attention_gradient = grad_middle.astype(jnp.bfloat16)
        total_output = total_output + jnp.einsum(
            "xab,xac->bc", context_rows, attention_gradient, preferred_element_type=jnp.float32
        )
        grad_context = jnp.einsum(
            "pox,tx->pot", attention_gradient, output_reverse, preferred_element_type=jnp.float32
        ).astype(jnp.bfloat16)
        grad_heads = lax.all_to_all(
            grad_context, "head", split_axis=2, concat_axis=0, tiled=True
        ).reshape(shaped)
        grad_query, grad_key, grad_value = lax.map(
            lambda parts: attend_backward(*parts),
            (query, key_rows, value_rows, segment, logsums, grad_heads),
        )
        low_query = grad_query.reshape(count, length, width).astype(jnp.bfloat16)
        low_key = grad_key.reshape(count, length, width).astype(jnp.bfloat16)
        low_value = grad_value.reshape(count, length, width).astype(jnp.bfloat16)
        projection_gradient = jnp.stack([low_query, low_key, low_value], axis=2)
        attend_term = jnp.einsum(
            "eoy,eoxp->yxp",
            complete_normed,
            projection_gradient,
            preferred_element_type=jnp.float32,
        )
        total_attend = attend_term if total_attend is None else total_attend + attend_term
        grad_terms = jnp.einsum(
            "jbqn,iqn->jbi", projection_gradient, attend_reverse, preferred_element_type=jnp.float32
        )
        query_sum = jnp.sum(low_query.astype(jnp.float32), axis=(0, 1))
        value_sum = jnp.sum(low_value.astype(jnp.float32), axis=(0, 1))
        grad_normed_in = lax.psum_scatter(grad_terms, "head", scatter_dimension=0, tiled=True)
        zero_model = jnp.zeros((model,), jnp.float32)
        query_bias_grad = lax.dynamic_update_slice_in_dim(
            zero_model, query_sum, head_place * width, 0
        )
        value_bias_grad = lax.dynamic_update_slice_in_dim(
            zero_model, value_sum, head_place * width, 0
        )
        grad_input = grad_middle + norm_back(
            grad_normed_in, normed_first, factor_first, model_parameters[:, 0]
        )
        input_parts.append(grad_input.astype(jnp.bfloat16))
        columns = jnp.stack(
            [
                jnp.sum(grad_normed_in * normed_first, axis=(0, 1)),
                jnp.sum(grad_normed_in, axis=(0, 1)),
                query_bias_grad,
                value_bias_grad,
                jnp.sum(attention_gradient.astype(jnp.float32), axis=(0, 1)),
                jnp.sum(grad_normed_mid * normed_second, axis=(0, 1)),
                jnp.sum(grad_normed_mid, axis=(0, 1)),
                jnp.sum(branch_gradient.astype(jnp.float32), axis=(0, 1)),
            ],
            axis=1,
        )
        expand_bias_grad = (
            jnp.sum(preactivation_gradient.astype(jnp.float32), axis=(0, 1))
            .reshape(hidden_width // model, model)
            .T
        )
        total_vectors = total_vectors + jnp.concatenate([columns, expand_bias_grad], axis=1)
    grad_attend = lax.psum_scatter(total_attend, "batch", scatter_dimension=0, tiled=True)
    grad_output, grad_expand, grad_reduce, grad_vectors = (
        lax.psum_scatter(total_output, ("batch", "head"), scatter_dimension=0, tiled=True),
        lax.psum_scatter(total_expand, ("batch", "head"), scatter_dimension=0, tiled=True),
        lax.psum_scatter(total_reduce, ("batch", "head"), scatter_dimension=0, tiled=True),
        lax.psum_scatter(total_vectors, ("batch", "head"), scatter_dimension=0, tiled=True),
    )
    weights = (attend_weight, output_weight, expand_weight, reduce_weight, vectors)
    grads = (grad_attend, grad_output, grad_expand, grad_reduce, grad_vectors)
    firsts = (first_attend, first_output, first_expand, first_reduce, first_vectors)
    seconds = (second_attend, second_output, second_expand, second_reduce, second_vectors)
    adapted = [
        adapt(grads[number], firsts[number], seconds[number], weights[number])
        for number in range(5)
    ]
    weight_squares = jnp.concatenate(
        [
            jnp.stack([jnp.sum(weights[number] * weights[number]) for number in range(4)]),
            jnp.sum(vectors * vectors, axis=0),
        ]
    )
    update_squares = jnp.concatenate(
        [
            jnp.stack([jnp.sum(adapted[number][2] * adapted[number][2]) for number in range(4)]),
            jnp.sum(adapted[4][2] * adapted[4][2], axis=0),
        ]
    )
    weight_total, update_total = lax.psum((weight_squares, update_squares), ("batch", "head"))
    weight_norm = jnp.sqrt(weight_total)
    update_norm = jnp.sqrt(update_total)
    ratio = weight_norm / (update_norm + ADAM_EPS)
    masters = [weights[number] - RATE * ratio[number] * adapted[number][2] for number in range(4)]
    masters.append(vectors - RATE * ratio[4:][None, :] * adapted[4][2])
    trust_norms = jnp.log(jnp.stack([weight_norm, update_norm, ratio]))
    hidden_states = jnp.concatenate(hidden_parts, axis=0)
    input_gradient = jnp.concatenate(input_parts, axis=0)
    return (
        hidden_states,
        input_gradient,
        adapted[0][0],
        adapted[1][0],
        adapted[2][0],
        adapted[3][0],
        adapted[4][0],
        adapted[0][1],
        adapted[1][1],
        adapted[2][1],
        adapted[3][1],
        adapted[4][1],
        masters[0],
        masters[1],
        masters[2],
        masters[3],
        masters[4],
        trust_norms,
    )


def solution(mesh):
    return jax.shard_map(
        shards,
        mesh=mesh,
        in_specs=(
            P(("batch", "head"), None, None),
            P(("batch", "head"), None, None),
            P("batch", None),
            P("batch", None),
            P(("batch", "head"), None),
            P("batch", None, "head"),
            P(("batch", "head"), None),
            P(("batch", "head"), None),
            P(("batch", "head"), None),
            P(("batch", "head"), None),
            P("batch", None, "head"),
            P(("batch", "head"), None),
            P(("batch", "head"), None),
            P(("batch", "head"), None),
            P(("batch", "head"), None),
            P("batch", None, "head"),
            P(("batch", "head"), None),
            P(("batch", "head"), None),
            P(("batch", "head"), None),
            P(("batch", "head"), None),
        ),
        out_specs=(
            P(("batch", "head"), None, None),
            P(("batch", "head"), None, None),
            P("batch", None, "head"),
            P(("batch", "head"), None),
            P(("batch", "head"), None),
            P(("batch", "head"), None),
            P(("batch", "head"), None),
            P("batch", None, "head"),
            P(("batch", "head"), None),
            P(("batch", "head"), None),
            P(("batch", "head"), None),
            P(("batch", "head"), None),
            P("batch", None, "head"),
            P(("batch", "head"), None),
            P(("batch", "head"), None),
            P(("batch", "head"), None),
            P(("batch", "head"), None),
            P(),
        ),
        check_vma=False,
    )
```

profile of v0, /device:TPU:0, one launch (start us, length us, event | category | flops | bytes accessed | tf_op | source)
XLA Modules:
  0.0 1873.6 jit_solution(8618596038833699206)
XLA Ops:
  7.9 43.5 %all-gather = bf16[32,24,12]{1,2,0:T(8,128)(2,1)S(1)} all-gather(bf16[1,24,12]{1,2,0:T(8,128)(2,1)S(1)} %convert_bitcast_fusion), channel_id=1, replica_groups=mesh['batch'=8,'head'=4] {'batch','head'}, dimensions={0}, use_global_device_ids=true | all-gather | bytes 19008 | tf_op jit(solution)/shard_map/all_gather | solution.py:140
  69.4 35.7 %all_gather.16 = bf16[768,3,192]{2,1,0:T(4,128)(2,1)S(1)} all-gather(bf16[96,3,192]{2,1,0:T(4,128)(2,1)S(1)} %copy.171), channel_id=1, replica_groups=mesh['batch'=8,'head'=4] {'batch'}, dimensions={0}, use_global_device_ids=true | all-gather | bytes 995328 | tf_op jit(solution)/shard_map/all_gather | solution.py:133
  130.0 27.3 %all-gather.7.cloned.1.call-done = bf16[4,1024,768]{2,1,0:T(8,128)(2,1)} async-done(((bf16[1,1024,768]{2,1,0:T(8,128)(2,1)}), bf16[4,1024,768]{2,1,0:T(8,128)(2,1)}) %all-gather.7.cloned.1.call-update) | async-done | bytes 6291472 | tf_op jit(solution)/shard_map/all_gather | solution.py:208
  174.4 79.0 %while.107 = (s32[]{:T(128)}, bf16[4,1024,3,64]{1,3,2,0:T(8,128)(2,1)}, f32[4,2,3,512]{3,2,1,0:T(4,128)}, bf16[4,1024,3,64]{1,3,2,0:T(8,128)(2,1)}, s32[4,1024]{...) while((s32[]{:T(128)}, ...), condition=%wide.region_9.10_spmd, body=%wide.region_4.9_spmd.sunk | while | flops 421526528 | bytes 27177428 | solution.py:221
  177.5 14.1 while.114
  197.2 14.1 while.114
  216.9 14.1 while.114
  236.6 14.1 while.114
  259.7 78.8 %while.109 = (s32[]{:T(128)}, bf16[4,1024,3,64]{1,3,2,0:T(8,128)(2,1)}, f32[4,2,3,512]{3,2,1,0:T(4,128)}, bf16[4,1024,3,64]{1,3,2,0:T(8,128)(2,1)}, s32[4,1024]{...) while((s32[]{:T(128)}, ...), condition=%wide.region_21.22_spmd, body=%wide.region_16.21_spmd.sunk | while | flops 421526528 | bytes 27177428 | solution.py:221
  262.6 14.1 while.115
  282.4 14.1 while.115
  321.7 14.1 while.115
  396.2 15.5 convolution_add_fusion
  411.8 135.8 %reduce-scatter.18.cloned.1.call-done = f32[96,768]{1,0:T(8,128)} async-done(((f32[3072,768]{1,0:T(8,128)}), f32[96,768]{1,0:T(8,128)}) %reduce-scatter.18.cloned.1.call-update) | async-done | bytes 294928 | tf_op jit(solution)/shard_map/reduce_scatter | solution.py:342
  550.4 63.5 %all-gather.13.cloned.1.call-done = bf16[3072,768]{1,0:T(8,128)(2,1)} async-done(((bf16[96,768]{1,0:T(8,128)(2,1)}), bf16[3072,768]{1,0:T(8,128)(2,1)}) %all-gather.13.cloned.1.call-update) | async-done | bytes 4718608 | tf_op jit(solution)/shard_map/all_gather | solution.py:139
  614.0 17.1 convert_reduce_fusion.1
  650.2 16.7 convert_reduce_fusion
  775.2 259.5 %while.113 = (s32[]{:T(128)}, bf16[4,1024,3,64]{3,2,1,0:T(4,128)(2,1)}, bf16[4,1024,3,64]{1,3,2,0:T(8,128)(2,1)}, bf16[4,1024,3,64]{1,3,2,0:T(8,128)(2,1)}, bf16...) while((s32[]{:T(128)}, ...), condition=%wide.region_48.49_spmd, body=%wide.region_44.48_spmd.sunk | while | flops 1032879104 | bytes 102196112 | solution.py:287
  783.7 52.5 %while.117 = (s32[]{:T(128)}, f32[1024,3,64]{0,2,1:T(8,128)}, f32[1024,3,64]{0,2,1:T(8,128)}, bf16[2,512,3,64]{1,3,2,0:T(8,128)(2,1)}, s32[2]{0:T(128)S(1)}, /*i...) while((s32[]{:T(128)}, f32[1024,3,64]{0,2,1:T(8,128)}, ...), condition=%wide.region_47.47_spmd.clone, body=%wide.region_45.46_spmd.clone.sunk | while | flops 1032879104 | bytes 87351808 | solution.py:126
  848.7 52.3 %while.117 = (s32[]{:T(128)}, f32[1024,3,64]{0,2,1:T(8,128)}, f32[1024,3,64]{0,2,1:T(8,128)}, bf16[2,512,3,64]{1,3,2,0:T(8,128)(2,1)}, s32[2]{0:T(128)S(1)}, /*i...) while((s32[]{:T(128)}, f32[1024,3,64]{0,2,1:T(8,128)}, ...), condition=%wide.region_47.47_spmd.clone, body=%wide.region_45.46_spmd.clone.sunk | while | flops 1032879104 | bytes 87351808 | solution.py:126
  913.5 52.3 %while.117 = (s32[]{:T(128)}, f32[1024,3,64]{0,2,1:T(8,128)}, f32[1024,3,64]{0,2,1:T(8,128)}, bf16[2,512,3,64]{1,3,2,0:T(8,128)(2,1)}, s32[2]{0:T(128)S(1)}, /*i...) while((s32[]{:T(128)}, f32[1024,3,64]{0,2,1:T(8,128)}, ...), condition=%wide.region_47.47_spmd.clone, body=%wide.region_45.46_spmd.clone.sunk | while | flops 1032879104 | bytes 87351808 | solution.py:126
  978.3 52.3 %while.117 = (s32[]{:T(128)}, f32[1024,3,64]{0,2,1:T(8,128)}, f32[1024,3,64]{0,2,1:T(8,128)}, bf16[2,512,3,64]{1,3,2,0:T(8,128)(2,1)}, s32[2]{0:T(128)S(1)}, /*i...) while((s32[]{:T(128)}, f32[1024,3,64]{0,2,1:T(8,128)}, ...), condition=%wide.region_47.47_spmd.clone, body=%wide.region_45.46_spmd.clone.sunk | while | flops 1032879104 | bytes 87351808 | solution.py:126
  1052.3 259.3 %while.111 = (s32[]{:T(128)}, bf16[4,1024,3,64]{3,2,1,0:T(4,128)(2,1)}, bf16[4,1024,3,64]{1,3,2,0:T(8,128)(2,1)}, bf16[4,1024,3,64]{1,3,2,0:T(8,128)(2,1)}, bf16...) while((s32[]{:T(128)}, ...), condition=%wide.region_34.35_spmd, body=%wide.region_30.34_spmd.sunk | while | flops 1032879104 | bytes 102196112 | solution.py:287
  1060.7 52.3 %while.116 = (s32[]{:T(128)}, f32[1024,3,64]{0,2,1:T(8,128)}, f32[1024,3,64]{0,2,1:T(8,128)}, bf16[2,512,3,64]{1,3,2,0:T(8,128)(2,1)}, s32[2]{0:T(128)S(1)}, /*i...) while((s32[]{:T(128)}, f32[1024,3,64]{0,2,1:T(8,128)}, ...), condition=%wide.region_33.33_spmd.clone, body=%wide.region_31.32_spmd.clone.sunk | while | flops 1032879104 | bytes 87351808 | solution.py:126
  1125.5 52.3 %while.116 = (s32[]{:T(128)}, f32[1024,3,64]{0,2,1:T(8,128)}, f32[1024,3,64]{0,2,1:T(8,128)}, bf16[2,512,3,64]{1,3,2,0:T(8,128)(2,1)}, s32[2]{0:T(128)S(1)}, /*i...) while((s32[]{:T(128)}, f32[1024,3,64]{0,2,1:T(8,128)}, ...), condition=%wide.region_33.33_spmd.clone, body=%wide.region_31.32_spmd.clone.sunk | while | flops 1032879104 | bytes 87351808 | solution.py:126
  1190.3 52.3 %while.116 = (s32[]{:T(128)}, f32[1024,3,64]{0,2,1:T(8,128)}, f32[1024,3,64]{0,2,1:T(8,128)}, bf16[2,512,3,64]{1,3,2,0:T(8,128)(2,1)}, s32[2]{0:T(128)S(1)}, /*i...) while((s32[]{:T(128)}, f32[1024,3,64]{0,2,1:T(8,128)}, ...), condition=%wide.region_33.33_spmd.clone, body=%wide.region_31.32_spmd.clone.sunk | while | flops 1032879104 | bytes 87351808 | solution.py:126
  1255.1 52.3 %while.116 = (s32[]{:T(128)}, f32[1024,3,64]{0,2,1:T(8,128)}, f32[1024,3,64]{0,2,1:T(8,128)}, bf16[2,512,3,64]{1,3,2,0:T(8,128)(2,1)}, s32[2]{0:T(128)S(1)}, /*i...) while((s32[]{:T(128)}, f32[1024,3,64]{0,2,1:T(8,128)}, ...), condition=%wide.region_33.33_spmd.clone, body=%wide.region_31.32_spmd.clone.sunk | while | flops 1032879104 | bytes 87351808 | solution.py:126
  1424.8 118.6 %reduce-scatter.16.cloned.1.call-done = f32[24,3072]{1,0:T(8,128)} async-done(((f32[768,3072]{1,0:T(8,128)}), f32[24,3072]{1,0:T(8,128)}) %reduce-scatter.16.cloned.1.call-update) | async-done | bytes 294928 | tf_op jit(solution)/shard_map/reduce_scatter | solution.py:341
  1546.2 97.9 %reduce-scatter.8.cloned.1.call-done = f32[1,1024,768]{1,2,0:T(8,128)} async-done(((f32[4,1024,768]{1,2,0:T(8,128)}), f32[1,1024,768]{1,2,0:T(8,128)}) %reduce-scatter.8.cloned.1.call-update) | async-done | bytes 3145744 | tf_op jit(solution)/shard_map/reduce_scatter | solution.py:307
  1649.6 96.4 %reduce-scatter.10.cloned.1.call-done = f32[1,1024,768]{1,2,0:T(8,128)} async-done(((f32[4,1024,768]{1,2,0:T(8,128)}), f32[1,1024,768]{1,2,0:T(8,128)}) %reduce-scatter.10.cloned.1.call-update) | async-done | bytes 3145744 | tf_op jit(solution)/shard_map/reduce_scatter | solution.py:307
  1754.9 39.8 %all-reduce = f32[768,12]{0,1:T(8,128)S(1)} all-reduce(f32[768,12]{0,1:T(8,128)S(1)} %add.511), channel_id=8, replica_groups=mesh['batch'=8,'head'=4] {'batch','head'}, use_global_device_ids=true, to_apply=%region_74.75.clone | all-reduce | flops 9216 | bytes 73728
  1805.5 40.9 %all-reduce.1 = (f32[16]{0:T(128)S(1)}, f32[16]{0:T(128)S(1)}) all-reduce(f32[16]{0:T(128)S(1)} %concatenate.23, f32[16]{0:T(128)S(1)} %concatenate.22), channel_id=1, replica_groups=mesh['batch'=8,'head'=4] {'batch','head'}, use_global_device_ids=true, to_apply=%region_86.87 | all-reduce | flops 32 | bytes 256 | tf_op jit(solution)/shard_map/psum | solution.py:365
  (1209 shorter events, 1065.7 us)
Async XLA Ops:
  7.2 112.4 %all-gather.15.cloned.1.call-start = ((), (), s32[]{:S(2)}) async-start(), calls=%async_computation.14 | async-start | bytes 7864320 | tf_op jit(solution)/shard_map/all_gather | solution.py:208
  66.0 91.2 %all-gather.7.cloned.1.call-start = ((), (), s32[]{:S(2)}) async-start(), calls=%async_computation.10 | async-start | bytes 7864320 | tf_op jit(solution)/shard_map/all_gather | solution.py:208
  67.7 275.0 %all-gather.9.cloned.1.call-start = ((), (), s32[]{:S(2)}) async-start(), calls=%async_computation.11 | async-start | bytes 1216512 | tf_op jit(solution)/shard_map/all_gather | solution.py:137
  68.4 300.0 %all-gather.11.cloned.1.call-start = ((), (), s32[]{:S(2)}) async-start(), calls=%async_computation.12 | async-start | bytes 4866048 | tf_op jit(solution)/shard_map/all_gather | solution.py:138
  253.3 85.1 %all-to-all-start = ((bf16[4,1024,192]{1,2,0:T(8,128)(2,1)}), bf16[4,1024,192]{1,2,0:T(8,128)(2,1)}, u32[]{:S(2)}, u32[]{:S(2)}) async-start(bf16[4,1024,192]{1,2,0:T(8,128)(2,1)} %bitcast.47), calls=%async_computation | async-start | bytes 3145728 | tf_op jit(solution)/shard_map/all_to_all | solution.py:225
  338.5 23.8 %all-to-all-start.1 = ((bf16[4,1024,192]{1,2,0:T(8,128)(2,1)}), bf16[4,1024,192]{1,2,0:T(8,128)(2,1)S(1)}, u32[]{:S(2)}, u32[]{:S(2)}) async-start(bf16[4,1024,192]{1,2,0:T(8,128)(2,1)} %bitcast.62), calls=%async_computation.1 | async-start | bytes 3145728 | tf_op jit(solution)/shard_map/all_to_all | solution.py:225
  342.2 205.4 %reduce-scatter.18.cloned.1.call-start = ((), (), s32[]{:S(2)}) async-start(), calls=%async_computation.20 | async-start | bytes 9732096 | tf_op jit(solution)/shard_map/reduce_scatter | solution.py:342
  346.2 335.0 %copy-start.64 = (f32[1024]{0:T(1024)}, f32[1024]{0:T(1024)S(1)}, u32[]{:S(2)}) copy-start(f32[1024]{0:T(1024)S(1)} %broadcast_multiply_fusion.12) | copy-start | bytes 12292
  348.2 333.0 %copy-start.68 = (f32[1024]{0:T(1024)}, f32[1024]{0:T(1024)S(1)}, u32[]{:S(2)}) copy-start(f32[1024]{0:T(1024)S(1)} %add_rsqrt_fusion.2) | copy-start | bytes 12292
  366.4 322.0 %copy-start.62 = (f32[1024]{0:T(1024)}, f32[1024]{0:T(1024)S(1)}, u32[]{:S(2)}) copy-start(f32[1024]{0:T(1024)S(1)} %broadcast_multiply_fusion.10) | copy-start | bytes 12292
  368.4 320.0 %copy-start.66 = (f32[1024]{0:T(1024)}, f32[1024]{0:T(1024)S(1)}, u32[]{:S(2)}) copy-start(f32[1024]{0:T(1024)S(1)} %add_rsqrt_fusion) | copy-start | bytes 12292
  411.7 135.9 %copy-start.58 = (f32[96,768]{1,0:T(8,128)S(1)}, f32[96,768]{1,0:T(8,128)}, u32[]{:S(2)}) copy-start(f32[96,768]{1,0:T(8,128)} %param.44) | copy-start | bytes 884740
  411.8 202.2 %all-gather.13.cloned.1.call-start = ((), (), s32[]{:S(2)}) async-start(), calls=%async_computation.13 | async-start | bytes 4866048 | tf_op jit(solution)/shard_map/all_gather | solution.py:139
  718.2 41.6 %all-to-all-start.3 = ((bf16[4,2,98304]{2,1,0:T(2,128)(2,1)}), bf16[4,2,98304]{2,1,0:T(2,128)(2,1)}, u32[]{:S(2)}, u32[]{:S(2)}) async-start(bf16[4,2,98304]{2,1,0:T(2,128)(2,1)} %reshape.1190), calls=%async_computation.4 | async-start | bytes 3145728 | tf_op jit(solution)/shard_map/all_to_all | solution.py:284
  722.5 697.0 %reduce-scatter.14.cloned.1.call-start = ((), (), s32[]{:S(2)}) async-start(), calls=%async_computation.18 | async-start | bytes 2433024 | tf_op jit(solution)/shard_map/reduce_scatter | solution.py:340
  759.8 281.6 %all-to-all-start.2 = ((bf16[4,2,98304]{2,1,0:T(2,128)(2,1)}), bf16[4,2,98304]{2,1,0:T(2,128)(2,1)}, u32[]{:S(2)}, u32[]{:S(2)}) async-start(bf16[4,2,98304]{2,1,0:T(2,128)(2,1)} %reshape.1192), calls=%async_computation.2 | async-start | bytes 3145728 | tf_op jit(solution)/shard_map/all_to_all | solution.py:284
  764.6 657.3 %reduce-scatter.12.cloned.1.call-start = ((), (), s32[]{:S(2)}) async-start(), calls=%async_computation.17 | async-start | bytes 2654208 | tf_op jit(solution)/shard_map/reduce_scatter | solution.py:338
  1333.8 209.5 %reduce-scatter.16.cloned.1.call-start = ((), (), s32[]{:S(2)}) async-start(), calls=%async_computation.19 | async-start | bytes 9732096 | tf_op jit(solution)/shard_map/reduce_scatter | solution.py:341
  1352.5 291.6 %reduce-scatter.8.cloned.1.call-start = ((), (), s32[]{:S(2)}) async-start(), calls=%async_computation.15 | async-start | bytes 15728640 | tf_op jit(solution)/shard_map/reduce_scatter | solution.py:307
  1362.8 383.2 %reduce-scatter.10.cloned.1.call-start = ((), (), s32[]{:S(2)}) async-start(), calls=%async_computation.16 | async-start | bytes 15728640 | tf_op jit(solution)/shard_map/reduce_scatter | solution.py:307
  1416.6 227.5 %copy-start.11 = (bf16[1,1024,768]{1,2,0:T(8,128)(2,1)S(1)}, bf16[1,1024,768]{1,2,0:T(8,128)(2,1)}, u32[]{:S(2)}) copy-start(bf16[1,1024,768]{1,2,0:T(8,128)(2,1)} %copy-done.9) | copy-start | bytes 4718596
  1416.6 227.5 %copy-start.73 = (f32[768]{0:T(1024)S(1)}, f32[768]{0:T(1024)}, u32[]{:S(2)}) copy-start(f32[768]{0:T(1024)} %copy-done.72) | copy-start | bytes 9220
  1416.6 227.5 %copy-start.75 = (f32[1024]{0:T(1024)S(1)}, f32[1024]{0:T(1024)}, u32[]{:S(2)}) copy-start(f32[1024]{0:T(1024)} %copy-done.74) | copy-start | bytes 12292
  1416.6 227.5 %copy-start.80 = (f32[1024]{0:T(1024)S(1)}, f32[1024]{0:T(1024)}, u32[]{:S(2)}) copy-start(f32[1024]{0:T(1024)} %copy-done.79) | copy-start | bytes 12292
  1417.9 128.3 %copy-start.95 = (f32[768,1]{0,1:T(1,128)}, f32[768,1]{0,1:T(1,128)S(1)}, u32[]{:S(2)}) copy-start(f32[768,1]{0,1:T(1,128)S(1)} %dynamic_update_slice.69) | copy-start | bytes 9220
  1419.1 127.1 %copy-start.96 = (f32[768,1]{0,1:T(1,128)}, f32[768,1]{0,1:T(1,128)S(1)}, u32[]{:S(2)}) copy-start(f32[768,1]{0,1:T(1,128)S(1)} %dynamic_update_slice.70) | copy-start | bytes 9220
  1424.8 321.2 %copy-start.8 = (bf16[1,1024,768]{1,2,0:T(8,128)(2,1)S(1)}, bf16[1,1024,768]{1,2,0:T(8,128)(2,1)}, u32[]{:S(2)}) copy-start(bf16[1,1024,768]{1,2,0:T(8,128)(2,1)} %copy-done.6) | copy-start | bytes 4718596
  1424.8 321.2 %copy-start.71 = (f32[1024]{0:T(1024)S(1)}, f32[1024]{0:T(1024)}, u32[]{:S(2)}) copy-start(f32[1024]{0:T(1024)} %copy-done.70) | copy-start | bytes 12292
  1424.8 321.2 %copy-start.78 = (f32[1024]{0:T(1024)S(1)}, f32[1024]{0:T(1024)}, u32[]{:S(2)}) copy-start(f32[1024]{0:T(1024)} %copy-done.77) | copy-start | bytes 12292
  1649.6 145.2 %copy-start.76 = (f32[24,12]{0,1:T(8,128)S(1)}, f32[24,12]{0,1:T(8,128)}, u32[]{:S(2)}) copy-start(f32[24,12]{0,1:T(8,128)} %param.45) | copy-start | bytes 3460
  1795.7 69.9 %copy-start.81 = (f32[24,12]{0,1:T(8,128)}, f32[24,12]{0,1:T(8,128)S(1)}, u32[]{:S(2)}) copy-start(f32[24,12]{0,1:T(8,128)S(1)} %get-tuple-element.826) | copy-start | bytes 3460
  1795.7 69.9 %copy-start.82 = (f32[24,12]{0,1:T(8,128)}, f32[24,12]{0,1:T(8,128)S(1)}, u32[]{:S(2)}) copy-start(f32[24,12]{0,1:T(8,128)S(1)} %get-tuple-element.827) | copy-start | bytes 3460
  (229 other events, 1167.7 us)
Sparse Core Ops, SparseCore 0:
  66.2 42.4 all-gather.14
  110.8 46.4 all-gather.6
  160.8 54.1 all-gather.8
  218.3 71.1 all-gather.10
  411.9 135.6 reduce-scatter.17
  551.4 62.5 all-gather.12
  759.9 99.2 reduce-scatter.13
  1333.9 68.9 reduce-scatter.11
  1408.8 134.4 reduce-scatter.15
  1546.0 98.0 reduce-scatter.7
  1646.9 99.0 reduce-scatter.9
where the time goes:
time: 1890 us; the launch traced here: 1870 us
  matrix products  563 us (30%)
  waiting for transfers between devices  554 us (29%)
  local copies, waits for them, and re-layouts  327 us (17%)
  other arithmetic  179 us (9%)
  blocking collectives  160 us (8%)
  loops' own time  55.1 us (3%)
    reduce_scatter x2, waiting for transfers between devices, shards(): lax.psum_scatter(grad_terms, 'head', scatter_dimension=0, tiled=True)  194 us
    reduce_scatter x1, waiting for transfers between devices, shards(): lax.psum_scatter(total_reduce, ('batch', 'head'), scatter_dimension=0, ti...  136 us
    reduce_scatter x1, waiting for transfers between devices, shards(): lax.psum_scatter(total_expand, ('batch', 'head'), scatter_dimension=0, ti...  119 us
    dot_general x32, matrix products, block_scores(): jnp.einsum('qhd,khd->hqk', query_block, key_rows, preferred_element_type=...  94.6 us
    dot_general x16, matrix products, one_block(): jnp.einsum('qhd,khd->hqk', grad_block, value_rows, preferred_element_type...  91.1 us
    dot_general x16, matrix products, one_block(): jnp.einsum('hqk,qhd->khd', low_probs, grad_block, preferred_element_type=...  78 us
    squeeze x48, local copies, waits for them, and re-layouts, shards(): lax.map(lambda parts: attend_forward(*parts), (query, key_rows, value_row...  68.4 us
    all_gather x1, waiting for transfers between devices, fetch(): lax.all_gather(reduce_weight.astype(jnp.bfloat16), ('batch', 'head'), axi...  63.5 us
  transfers between devices with their start and end apart: 15, of which 7 were waited for; matrix products, arithmetic and copies ran while one was open for 45% of the time, Pallas kernels for 0%

commit v1 on v0

v1 whole, which is shorter than its diff:
```python
import jax
import jax.numpy as jnp
from jax import lax
from jax.experimental import pallas as pl
from jax.experimental.pallas import tpu as pltpu
from jax.sharding import PartitionSpec as P

HEAD_DIM = 64
THOUGHT_TOKENS = 8
STEP = 6
PARTS = 32
SPAN = 256
BLOCK = 128

NORM_EPS = 1e-05
NEGATIVE = -1e30
BETA = 0.5
RATE = 0.5
DECAY = 0.01
ADAM_EPS = 1e-06
AXES = ("batch", "head")
ROOT = 0.7978845608028654
CUBE = 0.044715
F32 = jnp.float32
BF16 = jnp.bfloat16
NT = (((1,), (1,)), ((), ()))
TN = (((0,), (0,)), ((), ()))


def dot(a, b, dims=(((1,), (0,)), ((), ()))):
    return lax.dot_general(a, b, dims, preferred_element_type=F32)


def params(grid=1, vmem=60):
    return pltpu.CompilerParams(
        dimension_semantics=("arbitrary",) * grid, vmem_limit_bytes=vmem * 1024 * 1024
    )


def cost(micros):
    return pl.CostEstimate(flops=int(micros * 0.29e9), bytes_accessed=1 << 18, transcendentals=0)


def whole(shape):
    return pl.BlockSpec(shape, lambda *_: (0,) * len(shape), pipeline_mode=pl.Buffered(1))


SCALARS = pl.BlockSpec(memory_space=pltpu.SMEM)


def row_facts(lengths, counts, mask, span):
    positions = jnp.arange(span, dtype=jnp.int32)
    ends = jnp.cumsum(lengths, axis=-1)
    starts = ends - lengths
    inside = (positions[None, :, None] >= starts[:, None, :]) & (
        positions[None, :, None] < ends[:, None, :]
    )
    start_of = jnp.sum(jnp.where(inside, starts[:, None, :], 0), axis=-1)
    passes = jnp.sum(jnp.where(inside, counts[:, None, :], 0), axis=-1)
    keep = (positions[None, :] - start_of >= THOUGHT_TOKENS * passes) & (mask > 0)
    return start_of, keep.astype(F32)


def windows(length):
    return [
        (low, max(0, low - SPAN), low + BLOCK - max(0, low - SPAN)) for low in range(0, length, BLOCK)
    ]


def fill_caps(start_ref, cap_ref, length):
    for number, (low, first, count) in enumerate(windows(length)):
        key = lax.broadcasted_iota(jnp.int32, (count, BLOCK), 0) + first
        query = lax.broadcasted_iota(jnp.int32, (count, BLOCK), 1) + low
        start = start_ref[0, :, low : low + BLOCK]
        allowed = (key <= query) & (key >= start)
        cap_ref[number, :count] = jnp.where(allowed, 3e38, NEGATIVE)


def cap_of(cap_ref, number, count):
    cap = cap_ref[number, :count]
    return jnp.concatenate([cap, cap], axis=1)


def for_heads(values):
    lane = lax.broadcasted_iota(jnp.int32, (1, 2 * HEAD_DIM), 1)
    return jnp.concatenate(
        [jnp.where(lane < HEAD_DIM, values, 0), jnp.where(lane >= HEAD_DIM, values, 0)], axis=0
    )


def of_heads(values):
    return jnp.concatenate([values[:HEAD_DIM, :BLOCK], values[HEAD_DIM:, BLOCK:]], axis=0)


def in_stages(units, ahead, behind, first, middle, last):
    started, worked = [first(unit) for unit in units[:ahead]], []
    for number, unit in enumerate(units):
        if number + ahead < len(units):
            started.append(first(units[number + ahead]))
        worked.append((unit, middle(unit, started.pop(0))))
        if len(worked) > behind:
            last(*worked.pop(0))
    for both in worked:
        last(*both)


def attend_forward_kernel(fresh, start_ref, q_ref, k_ref, v_ref, o_ref, log_ref, cap_ref):
    length = q_ref.shape[0]
    pl.when(fresh)(lambda: fill_caps(start_ref, cap_ref, length))
    value_t = v_ref[...].T

    def score(unit):
        _, (low, first, count) = unit
        query = for_heads(q_ref[low : low + BLOCK, :] * (HEAD_DIM**-0.5))
        return dot(k_ref[first : first + count, :], query, NT)

    def soften(unit, scores):
        number, (low, _, count) = unit
        scores = jnp.minimum(scores, cap_of(cap_ref, number, count))
        top = jnp.max(scores, axis=0, keepdims=True)
        grown = jnp.exp(scores - top)
        whole_sum = jnp.sum(grown, axis=0, keepdims=True)
        logs = top + jnp.log(whole_sum)
        log_ref[0, 0, :, low : low + BLOCK] = jnp.concatenate(
            [logs[:, :BLOCK], logs[:, BLOCK:]], axis=0
        )
        return grown.astype(BF16), 1.0 / whole_sum

    def mix(unit, found):
        _, (low, first, count) = unit
        grown, scale = found
        result = dot(value_t[:, first : first + count], grown) * scale
        o_ref[low : low + BLOCK, :] = of_heads(result).T.astype(BF16)

    in_stages(list(enumerate(windows(length))), 4, 1, score, soften, mix)


def attend_backward_kernel(
    fresh, start_ref, q_ref, k_ref, v_ref, o_ref, do_ref, log_ref, *rest
):
    d_ref, cap_ref = rest[-2:]
    length = q_ref.shape[0]
    pl.when(fresh)(lambda: fill_caps(start_ref, cap_ref, length))
    key_t = k_ref[...].T
    grad_key, grad_value = {}, {}

    def query_of(low):
        return for_heads(q_ref[low : low + BLOCK, :] * (HEAD_DIM**-0.5))

    def grad_of(low):
        return for_heads(do_ref[low : low + BLOCK, :])

    def side_by_side(values):
        return jnp.concatenate(values, axis=1)

    def score(unit):
        _, (low, first, count) = unit
        key, value = k_ref[first : first + count, :], v_ref[first : first + count, :]
        return dot(key, query_of(low), NT), dot(value, grad_of(low), NT)

    def soften(unit, found):
        number, (low, _, count) = unit
        scores, grad_probs = found
        product = do_ref[low : low + BLOCK, :].astype(F32) * o_ref[low : low + BLOCK, :].astype(F32)
        product = product.T
        inner = side_by_side([total(product[:HEAD_DIM]), total(product[HEAD_DIM:])])
        logs = side_by_side([log_ref[0, 0, h : h + 1, low : low + BLOCK] for h in range(2)])
        probs = jnp.exp(jnp.minimum(scores, cap_of(cap_ref, number, count)) - logs)
        return probs.astype(BF16), (probs * (grad_probs - inner)).astype(BF16)

    def mix(unit, found):
        _, (low, first, count) = unit
        probs, grad_scores = found
        terms = dot(probs, grad_of(low)), dot(grad_scores, query_of(low))
        grad_query = dot(key_t[:, first : first + count], grad_scores)
        d_ref[0, low : low + BLOCK, :] = (of_heads(grad_query).T * (HEAD_DIM**-0.5)).astype(BF16)
        for sums, term, place in ((grad_value, terms[0], 2), (grad_key, terms[1], 1)):
            for at in range(first, first + count, BLOCK):
                one = term[at - first : at - first + BLOCK]
                sums[at] = sums[at] + one if at in sums else one
            for at in list(sums):
                if at <= low - SPAN or low + BLOCK == length:
                    d_ref[place, at : at + BLOCK, :] = sums.pop(at).astype(BF16)

    in_stages(list(enumerate(windows(length))), 2, 0, score, soften, mix)


def attention_specs(length, pairs, low=0):
    pair = 2 * HEAD_DIM

    def at(i):
        return (i + low) // pairs, (i + low) % pairs

    def columns(n):
        return lambda i: (at(i)[0], n * pairs + at(i)[1])

    qkv = [pl.BlockSpec((length, pair), columns(n)) for n in range(3)]
    rows = pl.BlockSpec((length, pair), columns(0))
    logs = pl.BlockSpec((1, 1, 2, length), lambda i: (*at(i), 0, 0))
    start = pl.BlockSpec((1, 1, length), lambda i: (at(i)[0], 0, 0))
    return start, qkv, rows, logs, lambda i: (0, *at(i))


def attend_forward(start, qkv, length):
    tokens, model = qkv.shape[0], qkv.shape[1] // 3
    pairs = model // (2 * HEAD_DIM)
    rows = tokens // length
    start_spec, qkv_specs, row_spec, log_spec, _ = attention_specs(length, pairs)

    def kernel(*refs):
        attend_forward_kernel(pl.program_id(0) % pairs == 0, *refs)

    return pl.pallas_call(
        kernel,
        grid=(rows * pairs,),
        in_specs=[start_spec] + qkv_specs,
        out_specs=[row_spec, log_spec],
        out_shape=[
            jax.ShapeDtypeStruct((tokens, model), BF16),
            jax.ShapeDtypeStruct((rows, pairs, 2, length), F32),
        ],
        scratch_shapes=[pltpu.VMEM((length // BLOCK, SPAN + BLOCK, BLOCK), F32)],
        compiler_params=params(),
        cost_estimate=cost(18),
        name="attend_forward",
    )(start, qkv, qkv, qkv)


def attend_backward(start, qkv, out, grad, logs, length, low, high, before=None):
    tokens, model = out.shape
    pairs = model // (2 * HEAD_DIM)
    start_spec, qkv_specs, row_spec, log_spec, at = attention_specs(length, pairs, low)
    operands = [start, qkv, qkv, qkv, out, grad, logs]
    in_specs = [start_spec] + qkv_specs + [row_spec, row_spec, log_spec]
    aliases = {}
    if before is not None:
        aliases = {len(operands): 0}
        operands.append(before)
        in_specs.append(pl.BlockSpec(memory_space=pl.ANY))

    def kernel(*refs):
        fresh = (pl.program_id(0) == 0) | ((pl.program_id(0) + low) % pairs == 0)
        attend_backward_kernel(fresh, *refs)

    return pl.pallas_call(
        kernel,
        grid=(high - low,),
        in_specs=in_specs,
        out_specs=pl.BlockSpec((3, length, 2 * HEAD_DIM), at),
        out_shape=jax.ShapeDtypeStruct((3, tokens, model), BF16),
        scratch_shapes=[pltpu.VMEM((length // BLOCK, SPAN + BLOCK, BLOCK), F32)],
        input_output_aliases=aliases,
        compiler_params=params(),
        cost_estimate=cost(2.3 * (high - low)),
        name="attend_backward",
    )(*operands)


def normalize(values):
    centre = values - jnp.mean(values, axis=-1, keepdims=True)
    factor = lax.rsqrt(jnp.mean(centre * centre, axis=-1, keepdims=True) + NORM_EPS)
    return centre * factor, factor


def norm_back(inner, normed, factor):
    return factor * (
        inner
        - jnp.mean(inner, axis=-1, keepdims=True)
        - normed * jnp.mean(inner * normed, axis=-1, keepdims=True)
    )


def total(values):
    return jnp.sum(values, axis=0, keepdims=True)


def project_kernel(place_ref, x_ref, own_ref, other_ref, nl_ref, qkv_ref, w_ref, vec_ref, *, heads):
    slots, rows, flat = own_ref.shape
    rows -= -(-vec_ref.shape[0] // 16) * 16
    part, model = flat // 3, x_ref.shape[1]
    groups = bit_groups(2 * slots)
    place = place_ref[0]

    @pl.when(pl.program_id(0) == 0)
    def _():
        for here in range(heads):

            @pl.when(place % heads == here)
            def _(here=here):
                for bit, ref in enumerate((own_ref, other_ref)):
                    for slot in range(slots):
                        mask = mask_of(slot, groups) | bit
                        head = here ^ (mask % heads)
                        row = pl.multiple_of(((place ^ mask) // heads) * rows, rows)
                        for j in range(3):
                            low = j * model + head * part
                            w_ref[pl.ds(row, rows), low : low + part] = ref[
                                slot, :rows, j * part : (j + 1) * part
                            ]

        count, each = vec_ref.shape[0], model // (2 * slots)
        lane = lax.broadcasted_iota(jnp.int32, (1, model), 1)
        found = jnp.zeros((count, model), F32)
        for bit, ref in enumerate((own_ref, other_ref)):
            for slot in range(slots):
                device = place ^ (mask_of(slot, groups) | bit)
                piece = ref[slot, rows:, :128].astype(F32)[:count]
                piece = jnp.concatenate([piece] * (model // 128), axis=1)
                piece = pltpu.roll(piece, (device * each) % 128, 1)
                inside = (lane >= device * each) & (lane < (device + 1) * each)
                found = jnp.where(inside, piece, found)
        vec_ref[...] = found

    normed, _ = normalize(x_ref[...].astype(F32))
    low = (normed * vec_ref[0:1, :] + vec_ref[1:2, :]).astype(BF16)
    nl_ref[...] = low
    for j in range(3):
        side = slice(j * model, (j + 1) * model)
        result = dot(low, w_ref[:, side])
        if j != 1:
            result = result + vec_ref[2 + j // 2 : 3 + j // 2, :]
        qkv_ref[:, side] = result.astype(BF16)


def project(place, x, own, other, heads, cols, tile=512):
    tokens, model = x.shape
    row = pl.BlockSpec((tile, model), lambda i: (i, 0))
    return pl.pallas_call(
        lambda *refs: project_kernel(*refs, heads=heads),
        grid=(tokens // tile,),
        in_specs=[SCALARS, row, whole(own.shape), whole(other.shape)],
        out_specs=[
            row,
            pl.BlockSpec((tile, 3 * model), lambda i: (i, 0)),
            pl.BlockSpec((model, 3 * model), lambda i: (0, 0)),
            pl.BlockSpec((cols, model), lambda i: (0, 0)),
        ],
        out_shape=[
            jax.ShapeDtypeStruct((tokens, model), BF16),
            jax.ShapeDtypeStruct((tokens, 3 * model), BF16),
            jax.ShapeDtypeStruct((model, 3 * model), BF16),
            jax.ShapeDtypeStruct((cols, model), F32),
        ],
        compiler_params=params(),
        cost_estimate=cost(14),
        name="project",
    )(place, x, own, other)


class Late:
    def __init__(self, refs, scratch):
        (self.parts,) = refs
        self.expand, self.reduce, self.output, self.stage, self.sem = scratch
        self.model = self.output.shape[1]
        self.chunks = self.expand.shape[0]

    def copies(self):
        per = self.model // self.stage.shape[1]
        red = self.reduce.shape[0] // (2 * self.stage.shape[1])
        end = 2 * per + red
        for device in range(self.parts.shape[0]):
            row, bit = (device // 2) * per, device % 2
            for n in range(2):
                yield (
                    self.parts.at[device, n * per : (n + 1) * per],
                    self.expand.at[2 * bit + n, row : row + per],
                )
            yield (
                self.parts.at[device, 2 * per : end],
                self.reduce.at[device * red : (device + 1) * red],
            )
            yield (
                self.parts.at[device, end : end + self.stage.shape[2]],
                self.stage.at[bit, device // 2],
            )

    def load(self):
        copies = [pltpu.make_async_copy(a, b, self.sem) for a, b in self.copies()]
        for copy in copies:
            copy.start()
        for copy in copies:
            copy.wait()
        slots = self.stage.shape[1]
        per = self.model // slots
        for n in range(slots):
            both = [self.stage[bit, n, : per // 2, :].astype(F32) for bit in range(2)]
            self.output[n * per : (n + 1) * per, :] = jnp.concatenate(both, axis=0).astype(BF16)

    def reduce_rows(self, c):
        return self.reduce[c * self.model : (c + 1) * self.model, :]

    @staticmethod
    def specs():
        return [pl.BlockSpec(memory_space=pl.ANY)]

    @staticmethod
    def scratch(late, hidden):
        slots, _, model = late[0].shape
        slots //= 2
        return [
            pltpu.VMEM((hidden // model, model, model), BF16),
            pltpu.VMEM((hidden, model), BF16),
            pltpu.VMEM((model, model), BF16),
            pltpu.VMEM((2, slots, 32, model), BF16),
            pltpu.SemaphoreType.DMA,
        ]


def mlp_forward_kernel(*refs):
    late = Late(refs[:-16], refs[-5:])
    ctx_ref, x_ref, cot_ref, wt_ref, vec_ref = refs[-16:-11]
    hid_ref, mid_ref, nm_ref, act_ref, dg_ref, gb_ref = refs[-11:-5]
    model = late.model
    pl.when(pl.program_id(0) == 0)(late.load)
    middle = x_ref[...].astype(F32) + dot(ctx_ref[...], late.output[...]) + vec_ref[4:5, :]
    mid_ref[...] = middle
    gb_ref[...] = (cot_ref[...].astype(F32) * wt_ref[...]).astype(BF16)
    normed, _ = normalize(middle)
    low = (normed * vec_ref[5:6, :] + vec_ref[6:7, :]).astype(BF16)
    nm_ref[...] = low
    result = middle + vec_ref[7:8, :]
    for c in range(late.chunks):
        side = slice(c * model, (c + 1) * model)
        pre = dot(low, late.expand[c]) + vec_ref[8 + c : 9 + c, :]
        square = pre * pre
        half = 0.5 + 0.5 * jnp.tanh(pre * (ROOT + (ROOT * CUBE) * square))
        act = pre * half
        dg = half + act * (1.0 - half) * (2.0 * ROOT + (6.0 * ROOT * CUBE) * square)
        dg_ref[:, side] = dg.astype(BF16)
        act = act.astype(BF16)
        act_ref[:, side] = act
        result = result + dot(act, late.reduce_rows(c))
    hid_ref[...] = result.astype(BF16)


def mlp_forward(late, ctx, x, cot, wt, vec, hidden, tile=256):
    tokens, model = x.shape
    row = pl.BlockSpec((tile, model), lambda i: (i, 0))
    wide = pl.BlockSpec((tile, hidden), lambda i: (i, 0))
    one = pl.BlockSpec((tile, 1), lambda i: (i, 0))

    def shape(width, kind=BF16):
        return jax.ShapeDtypeStruct((tokens, width), kind)

    return pl.pallas_call(
        mlp_forward_kernel,
        grid=(tokens // tile,),
        in_specs=Late.specs() + [row, row, row, one, whole(vec.shape)],
        out_specs=[row, row, row, wide, wide, row],
        out_shape=[
            shape(model), shape(model, F32), shape(model), shape(hidden), shape(hidden), shape(model),
        ],
        scratch_shapes=Late.scratch(late, hidden),
        compiler_params=params(),
        cost_estimate=cost(40),
        name="mlp_forward",
    )(*late, ctx, x, cot, wt, vec)


def mlp_backward_kernel(*refs):
    late = Late(refs[:-15], refs[-5:])
    cot_ref, wt_ref, mid_ref, dg_ref, vec_ref = refs[-15:-10]
    gpre_ref, gm_ref, ga_ref, gc_ref, sum_ref = refs[-10:-5]
    model = late.model

    @pl.when(pl.program_id(0) == 0)
    def _():
        late.load()
        sum_ref[...] = jnp.zeros_like(sum_ref)

    grad_out = cot_ref[...].astype(F32) * wt_ref[...]
    branch = grad_out.astype(BF16)
    sum_ref[3:4, :] += total(branch.astype(F32))
    back = None
    for c in range(late.chunks):
        side = slice(c * model, (c + 1) * model)
        grad = (dot(branch, late.reduce_rows(c), NT) * dg_ref[:, side].astype(F32)).astype(BF16)
        gpre_ref[:, side] = grad
        sum_ref[4 + c : 5 + c, :] += total(grad.astype(F32))
        term = dot(grad, late.expand[c], NT)
        back = term if back is None else back + term
    normed, factor = normalize(mid_ref[...])
    sum_ref[1:2, :] += total(back * normed)
    sum_ref[2:3, :] += total(back)
    grad_middle = grad_out + norm_back(back * vec_ref[5:6, :], normed, factor)
    gm_ref[...] = grad_middle
    low = grad_middle.astype(BF16)
    ga_ref[...] = low
    sum_ref[0:1, :] += total(low.astype(F32))
    gc_ref[...] = dot(low, late.output[...], NT).astype(BF16)


def mlp_backward(late, cot, wt, mid, dg, vec, tile=256):
    tokens, model = cot.shape
    hidden = dg.shape[1]
    row = pl.BlockSpec((tile, model), lambda i: (i, 0))
    wide = pl.BlockSpec((tile, hidden), lambda i: (i, 0))
    one = pl.BlockSpec((tile, 1), lambda i: (i, 0))

    def shape(width, kind=BF16):
        return jax.ShapeDtypeStruct((tokens, width), kind)

    return pl.pallas_call(
        mlp_backward_kernel,
        grid=(tokens // tile,),
        in_specs=Late.specs() + [row, one, row, wide, whole(vec.shape)],
        out_specs=[wide, row, row, row, pl.BlockSpec((8, model), lambda i: (0, 0))],
        out_shape=[
            shape(hidden), shape(model, F32), shape(model), shape(model),
            jax.ShapeDtypeStruct((8, model), F32),
        ],
        scratch_shapes=Late.scratch(late, hidden),
        compiler_params=params(),
        cost_estimate=cost(36),
        name="mlp_backward",
    )(*late, cot, wt, mid, dg, vec)


def put_parts(place, outs, pieces, turn=False):
    groups = bit_groups(2 * outs[0].shape[0])
    for bit in range(2):

        @pl.when(place % 2 == bit)
        def _(bit=bit):
            for device, index, value in pieces:
                mask = place ^ device
                slot = slot_of(turned(mask, groups) if turn else mask, groups)
                outs[(device % 2) ^ bit][(slot,) + index] = value


def reduce_weight_grad_kernel(place_ref, a_ref, b_ref, *outs):
    slots, rows, _ = outs[0].shape
    result = dot(a_ref[...], b_ref[...], TN).astype(BF16)
    count = result.shape[0] // (2 * rows)
    for step in range(2 * slots // count):

        @pl.when(pl.program_id(0) == step)
        def _(step=step):
            for half in range(2):
                put_parts(
                    place_ref[0],
                    outs[half::2],
                    [
                        (
                            step * count + n,
                            (),
                            result[(2 * n + half) * rows : (2 * n + half + 1) * rows],
                        )
                        for n in range(count)
                    ],
                    half == 1,
                )


def outs_of(*shapes):
    return dict(
        out_specs=[pl.BlockSpec(shape, lambda *_: (0,) * len(shape)) for shape in shapes],
        out_shape=[jax.ShapeDtypeStruct(shape, BF16) for shape in shapes],
    )


def reduce_weight_grad(place, act, branch):
    tokens, model = branch.shape
    hidden = act.shape[1]
    shape = (PARTS // 2, hidden // PARTS // 2, model)
    found = pl.pallas_call(
        reduce_weight_grad_kernel,
        grid=(hidden // model,),
        in_specs=[SCALARS, pl.BlockSpec((tokens, model), lambda i: (0, i)), whole(branch.shape)],
        **outs_of(*[shape] * 4),
        compiler_params=params(),
        cost_estimate=cost(15),
        name="reduce_weight_grad",
    )(place, act, branch)
    return found[:2], found[2:]


def mid_weight_grad_kernel(place_ref, nm_ref, gpre_ref, ctx_ref, ga_ref, *outs):
    slots, rows, model = outs[0].shape
    per = model // slots
    step = pl.program_id(0)
    last = pl.num_programs(0) - 1
    place = place_ref[0]

    for c in range(4):

        @pl.when(step == c)
        def _(c=c):
            result = dot(nm_ref[...], gpre_ref[...], TN).astype(BF16)
            put_parts(
                place,
                outs[c % 2 :: 2],
                [
                    (2 * n + c // 2, (slice(0, per),), result[n * per : (n + 1) * per])
                    for n in range(slots)
                ],
                c % 2 == 1,
            )

    @pl.when(step == last)
    def _():
        result = dot(ctx_ref[...], ga_ref[...], TN)
        half = per // 2
        empty = jnp.zeros((rows - per - half, model), F32)
        put_parts(
            place,
            outs[::2],
            [
                (
                    n,
                    (slice(per, rows),),
                    jnp.concatenate([result[n * half : (n + 1) * half], empty], axis=0).astype(BF16),
                )
                for n in range(2 * slots)
            ],
        )


def mid_weight_grad(place, nm, gpre, ctx, ga):
    tokens, model = nm.shape
    hidden = gpre.shape[1]
    assert hidden == 4 * model
    slots, per = PARTS // 2, 2 * model // PARTS
    shapes = [(slots, per + 32, model), (slots, per, model)]
    found = pl.pallas_call(
        mid_weight_grad_kernel,
        grid=(5,),
        in_specs=[
            SCALARS,
            whole(nm.shape),
            pl.BlockSpec((tokens, model), lambda i: (0, jnp.minimum(i, 3))),
            whole(ctx.shape),
            whole(ga.shape),
        ],
        **outs_of(*shapes * 2),
        compiler_params=params(),
        cost_estimate=cost(19),
        name="mid_weight_grad",
    )(place, nm, gpre, ctx, ga)
    return found[:2], found[2:]


def attend_weight_grad_kernel(place_ref, a_ref, b_ref, keep_ref, send_ref, *, heads):
    slots, rows, flat = keep_ref.shape
    part = flat // 3
    result = dot(a_ref[...], b_ref[0], TN).astype(BF16)
    for j in range(3):

        @pl.when(pl.program_id(0) == j)
        def _(j=j):
            put_parts(
                place_ref[0],
                (keep_ref, send_ref),
                [
                    (
                        d,
                        (slice(None), slice(j * part, (j + 1) * part)),
                        result[
                            d // heads * rows : (d // heads + 1) * rows,
                            d % heads * part : (d % heads + 1) * part,
                        ],
                    )
                    for d in range(2 * slots)
                ],
            )


def attend_weight_grad(place, nl, d_qkv, heads):
    tokens, model = nl.shape
    return pl.pallas_call(
        lambda *refs: attend_weight_grad_kernel(*refs, heads=heads),
        grid=(3,),
        in_specs=[SCALARS, whole(nl.shape), pl.BlockSpec((1, tokens, model), lambda j: (j, 0, 0))],
        **outs_of(*[(PARTS // 2, model * heads // PARTS, 3 * model // heads)] * 2),
        compiler_params=params(),
        cost_estimate=cost(13),
        name="attend_weight_grad",
    )(place, nl, d_qkv)


def input_grad_kernel(d_ref, x_ref, gm_ref, w_ref, vec_ref, mid_ref, out_ref, sum_ref):
    model = x_ref.shape[1]

    @pl.when(pl.program_id(0) == 0)
    def _():
        sum_ref[:4, :] = jnp.zeros((4, model), F32)
        sum_ref[4:, :] = mid_ref[...]

    back = None
    for j in range(3):
        term = dot(d_ref[j], w_ref[:, j * model : (j + 1) * model], NT)
        back = term if back is None else back + term
    normed, factor = normalize(x_ref[...].astype(F32))
    sum_ref[0:1, :] += total(back * normed)
    sum_ref[1:2, :] += total(back)
    sum_ref[2:3, :] += total(d_ref[0].astype(F32))
    sum_ref[3:4, :] += total(d_ref[2].astype(F32))
    out_ref[...] = (gm_ref[...] + norm_back(back * vec_ref[0:1, :], normed, factor)).astype(BF16)


def input_grad(d_qkv, x, gm, w, vec, mid_sums, tile=512):
    tokens, model = x.shape
    row = pl.BlockSpec((tile, model), lambda i: (i, 0))
    return pl.pallas_call(
        input_grad_kernel,
        grid=(tokens // tile,),
        in_specs=[
            pl.BlockSpec((3, tile, model), lambda i: (0, i, 0)), row, row,
            whole(w.shape), whole(vec.shape), whole(mid_sums.shape),
        ],
        out_specs=[row, pl.BlockSpec(vec.shape, lambda i: (0, 0))],
        out_shape=[
            jax.ShapeDtypeStruct((tokens, model), BF16), jax.ShapeDtypeStruct(vec.shape, F32),
        ],
        compiler_params=params(),
        cost_estimate=cost(16),
        name="input_grad",
    )(d_qkv, x, gm, w, vec, mid_sums)


def bit_groups(count):
    bits = count.bit_length() - 1
    assert count == 1 << bits
    return [(0, 1)] + [(low, min(2, bits - low)) for low in range(1, bits, 2)]


def slot_of(mask, groups):
    slot = 0
    for low, width in groups[1:]:
        slot = slot * (1 << width) + ((mask >> low) & ((1 << width) - 1))
    return slot


def mask_of(slot, groups):
    mask = 0
    for low, width in groups[:0:-1]:
        mask |= (slot & ((1 << width) - 1)) << low
        slot >>= width
    return mask


def swap(value, mask):
    count = lax.axis_size("batch") * lax.axis_size("head")
    return lax.ppermute(value, AXES, [(i, i ^ mask) for i in range(count)])


def spread(piece, group):
    low, width = group
    return [piece] + [swap(piece, step << low) for step in range(1, 1 << width)]


def join(parts):
    return jnp.concatenate(parts, axis=0)


def gather_far(piece, groups):
    piece = piece[None]
    for group in groups[:1:-1]:
        piece = join(spread(piece, group))
    return piece


def ordered(*values):
    return lax.optimization_barrier(values)


class Halves:
    def __init__(self, keep, send, groups):
        self.groups = groups
        self.bits = [2 << groups[1][0], 1 << groups[1][0]]
        self.terms = [[kept, swap(sent, 1)] for kept, sent in zip(keep, send)]
        self.count = keep[0].shape[0]

    def flat(self):
        return [t for terms in self.terms for t in terms]

    def set(self, flat):
        count = len(self.terms[0])
        self.terms = [list(flat[:count]), list(flat[count:])]

    def sends(self):
        self.count //= 2
        here = slice(self.count, 2 * self.count)
        return [added([t[here] for t in terms]).astype(BF16) for terms in self.terms]

    def receive(self, sends):
        received = [swap(send, bit) for send, bit in zip(sends, self.bits)]
        self.bits = self.bits[::-1]
        return received

    def add(self, received):
        self.terms = [terms + [one] for terms, one in zip(self.terms, received)]

    def at(self, slot):
        return jnp.concatenate([added([t[slot] for t in terms]) for terms in self.terms], axis=0)

    def last_sends(self):
        return [self.at(slot).astype(BF16) for slot in range(1, self.count)]

    def last_receive(self, sends):
        return [swap(send, (n + 1) << self.groups[2][0]) for n, send in enumerate(sends)]

    def finish(self, received):
        return added([self.at(0), *received])


class Whole:
    def __init__(self, keep, send, groups):
        self.groups = groups
        self.terms = [keep, swap(send, 1)]
        self.count = keep.shape[0]

    def sends(self):
        self.count //= 4
        return [
            added([t[n * self.count : (n + 1) * self.count] for t in self.terms]).astype(BF16)
            for n in range(1, 4)
        ]

    def receive(self, sends):
        return [swap(send, (n + 1) << self.groups[1][0]) for n, send in enumerate(sends)]

    def last_sends(self):
        return [added([t[n] for t in self.terms]).astype(BF16) for n in range(1, self.count)]

    def last_receive(self, sends):
        return [swap(send, (n + 1) << self.groups[2][0]) for n, send in enumerate(sends)]

    def finish(self, received):
        return added([added([t[0] for t in self.terms]), *received])


def added(terms):
    return sum(term.astype(F32) for term in terms)


def scatter(keep, send, groups):
    terms = [keep, swap(send, 1)]
    for low, width in groups[1:]:
        count = 1 << width
        terms = [t.reshape((count, -1) + t.shape[1:]) for t in terms]
        sends = [added([t[step] for t in terms]).astype(BF16) for step in range(1, count)]
        terms = [added([t[0] for t in terms])]
        terms += [swap(send, (n + 1) << low) for n, send in enumerate(sends)]
    return added(terms)[0]


def all_sum(value, groups):
    for low, width in groups:
        value = sum([swap(value, s << low) for s in range(1, 1 << width)], value)
    return value


def turned(mask, groups):
    low = groups[1][0]
    both = (mask >> low) & 3
    return mask ^ ((both ^ (both >> 1) ^ ((both & 1) << 1)) << low)


def slot_masks(groups, turn=False):
    masks = [mask_of(slot, groups) for slot in range(1 << sum(width for _, width in groups[1:]))]
    return [turned(mask, groups) for mask in masks] if turn else masks


def in_order(parts, masks, place):
    found = [mask for part in masks for mask in part]
    slots = [0] * len(found)
    for slot, mask in enumerate(found):
        slots[mask] = slot
    devices = jnp.arange(len(found), dtype=jnp.int32)
    return jnp.take(join(parts), jnp.asarray(slots, jnp.int32)[place ^ devices], axis=0)


def by_slot(parts, place, groups):
    masks = jnp.asarray(slot_masks(groups), jnp.int32)
    return [jnp.take(parts, place ^ (masks | bit), axis=0) for bit in range(2)]


def adapt_kernel(rows, *refs):
    count = len(rows)
    inputs, outputs = refs[: 4 * count + 1], refs[4 * count + 1 :]
    sum_ref = outputs[-1]
    sum_ref[...] = inputs[-1][...]
    half = sum_ref.shape[0] // 2
    correct = 1.0 - BETA**STEP
    for number, row in enumerate(rows):
        grad_ref, first_ref, second_ref, weight_ref = inputs[4 * number : 4 * number + 4]
        moment_ref, square_ref, update_ref = outputs[3 * number : 3 * number + 3]
        planes = weight_ref.shape[0] if len(weight_ref.shape) == 3 else 1
        width = grad_ref.shape[1] // planes
        norms = []
        for n in range(planes):
            at = n if len(weight_ref.shape) == 3 else Ellipsis
            grad = grad_ref[:, n * width : (n + 1) * width]
            moment = BETA * first_ref[at] + (1.0 - BETA) * grad
            square = BETA * second_ref[at] + (1.0 - BETA) * grad * grad
            weight = weight_ref[at]
            update = moment / correct / (jnp.sqrt(square / correct) + ADAM_EPS) + DECAY * weight
            moment_ref[at] = moment
            square_ref[at] = square
            update_ref[at] = update
            norms.append([jnp.sum(v * v, axis=1, keepdims=True) for v in (weight, update)])
        for n in range(2):
            norm = sum(both[n] for both in norms)
            if row < 4:
                norm = total(norm)
            place = n * half + row
            sum_ref[place : place + norm.shape[0], :] = jnp.broadcast_to(norm, (norm.shape[0], 128))


def adapt(states, rows, sums=None):
    if sums is None:
        sums = jnp.zeros((32, 128), F32)
    operands = [array for state in states for array in state] + [sums]
    shapes = [state[3].shape for state in states for _ in range(3)] + [sums.shape]
    *found, sums = pl.pallas_call(
        lambda *refs: adapt_kernel(rows, *refs),
        grid=(1,),
        in_specs=[whole(a.shape) for a in operands],
        out_specs=[pl.BlockSpec(s, lambda *_, n=len(s): (0,) * n) for s in shapes],
        out_shape=[jax.ShapeDtypeStruct(s, F32) for s in shapes],
        compiler_params=params(),
        cost_estimate=cost(4),
        name="adapt",
    )(*operands)
    return [found[3 * n : 3 * n + 3] for n in range(len(states))], sums


def master_kernel(sum_ref, *refs):
    *refs, trust_ref = refs
    count = len(refs) // 3
    half = sum_ref.shape[0] // 2
    norms = [jnp.sqrt(sum_ref[n * half : (n + 1) * half, :]) for n in range(2)]
    ratio = norms[0] / (norms[1] + ADAM_EPS)
    row = lax.broadcasted_iota(jnp.int32, ratio.shape, 0)
    lane = lax.broadcasted_iota(jnp.int32, ratio.shape, 1)
    for n, value in enumerate([*norms, ratio]):
        line = jnp.log(total(jnp.where(row == lane, value, 0.0)))
        trust_ref[n : n + 1, :] = line[:, : trust_ref.shape[1]]
    for n in range(count):
        update_ref, weight_ref, out_ref = refs[n], refs[count + n], refs[2 * count + n]
        scale = RATE * (ratio[n : n + 1, :1] if n < 4 else ratio[4:, :1])
        for at in range(weight_ref.shape[0]) if len(weight_ref.shape) == 3 else [Ellipsis]:
            out_ref[at] = weight_ref[at] - scale * update_ref[at]


def master(sums, updates, weights):
    arrays = [sums, *updates, *weights]
    shapes = [a.shape for a in weights] + [(3, sums.shape[0] // 2)]
    return pl.pallas_call(
        master_kernel,
        grid=(1,),
        in_specs=[whole(a.shape) for a in arrays],
        out_specs=[pl.BlockSpec(s, lambda *_, n=len(s): (0,) * n) for s in shapes],
        out_shape=[jax.ShapeDtypeStruct(s, F32) for s in shapes],
        compiler_params=params(),
        cost_estimate=cost(3),
        name="master",
    )(*arrays)


def halves(parts, groups):
    return by_slot(parts, jnp.int32(0), groups)


def by_index(keep, send, groups, turn=False):
    masks = slot_masks(groups, turn)
    return in_order([keep, send], [masks, [mask | 1 for mask in masks]], jnp.int32(0))


def join_heads(pieces):
    nb, nh, rows, flat = pieces.shape
    wider = nb * nh // PARTS
    parts = pieces.reshape(nb // wider, wider, nh, rows, flat).transpose(0, 2, 1, 3, 4)
    return parts.reshape(PARTS, wider * rows, flat)


def join_parts(parts, nh):
    count = lax.axis_size("batch") * lax.axis_size("head")
    wider = count // PARTS
    _, rows, flat = parts.shape
    parts = parts.reshape(PARTS // nh, nh, wider, rows // wider, flat).transpose(0, 2, 1, 3, 4)
    return parts.reshape(count, rows // wider, flat)


def shards(
    block_input,
    cotangent,
    segment_lengths,
    thought_counts,
    packing_mask,
    attend_weight,
    output_weight,
    expand_weight,
    reduce_weight,
    vectors,
    first_attend,
    first_output,
    first_expand,
    first_reduce,
    first_vectors,
    second_attend,
    second_output,
    second_expand,
    second_reduce,
    second_vectors,
):
    nb, nh = lax.axis_size("batch"), lax.axis_size("head")
    count = nb * nh
    groups, kernel_groups = bit_groups(count), bit_groups(PARTS)
    same = count == PARTS
    place = (lax.axis_index("batch") * nh + lax.axis_index("head")).astype(jnp.int32)
    core = place % 2
    kernel_place = (place if same else jnp.zeros_like(place)).reshape(1)
    rows, length, model = block_input.shape
    tokens = rows * length
    hidden = expand_weight.shape[1]
    own_in, _, own_out = attend_weight.shape
    own = output_weight.shape[0]
    own_red = reduce_weight.shape[0]
    cols = vectors.shape[1]
    wide = hidden // model
    flat = 3 * own_out

    extra = jnp.pad(vectors.astype(BF16).T, ((0, -cols % 16), (0, flat - own)))
    piece = jnp.concatenate([attend_weight.astype(BF16).reshape(own_in, flat), extra], axis=0)
    attend_far = gather_far(piece, groups)

    blocks = expand_weight.astype(BF16).reshape(own, 2, wide // 2, model).transpose(1, 2, 0, 3)
    beside = swap(jnp.where(core == 0, blocks[1], blocks[0]), 1)
    mine = jnp.where(core == 0, blocks[0], blocks[1])
    piece = [
        jnp.concatenate(
            [jnp.where(core == 0, mine, beside), jnp.where(core == 0, beside, mine)], axis=1
        ).reshape(2 * own * (wide // 2), model),
        reduce_weight.astype(BF16),
        output_weight.astype(BF16),
    ]
    pad = -(own_red + own) % 16
    piece = jnp.concatenate(piece + [jnp.zeros((pad, model), BF16)], axis=0)
    late_all = lax.all_gather(piece, AXES, axis=0, tiled=False)
    attend_own = join(spread(attend_far, groups[1]))
    attend_other = swap(attend_own, 1)
    if not same:
        masks = slot_masks(groups)
        attend = in_order([attend_own, attend_other], [masks, [m | 1 for m in masks]], place)
        vec = attend[:, own_in:, :own].transpose(1, 0, 2).reshape(-1, PARTS, model // PARTS)
        vec = jnp.pad(vec.transpose(1, 0, 2), ((0, 0), (0, 0), (0, flat - model // PARTS)))
        attend = join_heads(attend[:, :own_in].reshape(nb, nh, own_in, flat))
        attend_own, attend_other = halves(
            jnp.concatenate([attend, vec], axis=1), kernel_groups
        )

    own_lengths = lax.dynamic_slice_in_dim(
        segment_lengths, lax.axis_index("head") * rows, rows, 0
    )
    own_counts = lax.dynamic_slice_in_dim(thought_counts, lax.axis_index("head") * rows, rows, 0)
    start_of, weight_rows = row_facts(own_lengths, own_counts, packing_mask, length)
    start_of = start_of.reshape(rows, 1, length)
    weight_rows = weight_rows.reshape(tokens, 1)

    x = block_input.reshape(tokens, model)
    cot = cotangent.reshape(tokens, model)
    normed_low, qkv, attend_low, vec = project(
        kernel_place, x, attend_own, attend_other, nh, cols
    )
    context, logs = attend_forward(start_of, qkv, length)
    if not same:
        late = late_all
        both, per = 2 * own, 2 * model // PARTS
        expand_low = (
            late[:, : both * wide // 2]
            .reshape(count // 2, 2, wide // 2, both, model)
            .transpose(1, 2, 0, 3, 4)
            .reshape(2, wide // 2, PARTS // 2, per, model)
            .transpose(2, 0, 1, 3, 4)
            .reshape(PARTS, per * (wide // 2), model)
        )
        low = both * wide // 2
        rest = [
            expand_low,
            late[:, low : low + own_red].reshape(PARTS, hidden // PARTS, model),
            late[:, low + own_red : low + own_red + own].reshape(PARTS, per // 2, model),
            jnp.zeros((PARTS, 8, model), BF16),
        ]
        late_all = jnp.concatenate(rest, axis=1)
    late = (late_all,)
    hidden_states, middle, middle_low, activated, slope, branch = mlp_forward(
        late, context, x, cot, weight_rows, vec, hidden
    )

    def for_devices(keep, send, split):
        parts = [by_index(*both, kernel_groups, n == 1) for n, both in enumerate(zip(keep, send))]
        return by_slot(split(jnp.concatenate(parts, axis=1)), place, groups)

    def split_mid(parts):
        per = 2 * model // PARTS
        expand = (
            jnp.stack([parts[:, :per], parts[:, per + 32 :]], axis=1)
            .reshape(PARTS // 2, 2, 2, per, model)
            .transpose(1, 2, 0, 3, 4)
            .reshape(2, 2, count // 2, 2 * own, model)
            .transpose(2, 0, 1, 3, 4)
            .reshape(count, 4 * own, model)
        )
        output = parts[:, per : per + per // 2].reshape(count, own, model)
        return jnp.concatenate([expand, output], axis=1)

    red_keep, red_send = reduce_weight_grad(kernel_place, activated, branch)
    if same:
        cot, *red_send = ordered(cot, *red_send)
        red = Halves(red_keep, red_send, groups)
    grad_pre, grad_middle, grad_attn, grad_context, mid_sums = mlp_backward(
        late, cot, weight_rows, middle, slope, vec
    )
    if same:
        grad_pre, *terms = ordered(grad_pre, *red.flat())
        red.set(terms)
        grad_pre, *sends = ordered(grad_pre, *red.sends())
        red_received = red.receive(sends)

    mid_keep, mid_send = mid_weight_grad(
        kernel_place, middle_low, grad_pre, context, grad_attn
    )
    if same:
        grad_context, *terms = ordered(grad_context, *mid_send, *red_received)
        mid = Halves(mid_keep, terms[:2], groups)
        red.add(terms[2:])
        grad_context, *sends = ordered(grad_context, *red.sends())
        red_received = red.receive(sends)

    pairs = model // (2 * HEAD_DIM)
    operands = (start_of, qkv, context, grad_context, logs, length)
    d_qkv = attend_backward(*operands, 0, pairs // 2)
    if same:
        d_qkv, *terms = ordered(d_qkv, *mid.flat(), *red_received)
        mid.set(terms[:4])
        red.add(terms[4:])
        d_qkv, *sends = ordered(d_qkv, *mid.sends(), *red.last_sends())
        mid_received = mid.receive(sends[:2])
        red_received = red.last_receive(sends[2:])
    d_qkv = attend_backward(*operands, pairs // 2, rows * pairs, d_qkv)
    if same:
        d_qkv, *terms = ordered(d_qkv, *mid_received, *red_received)
        mid.add(terms[:2])
        red_received = terms[2:]
        d_qkv, *sends = ordered(d_qkv, *mid.sends())
        mid_received = mid.receive(sends)
    att_keep, att_send = attend_weight_grad(kernel_place, normed_low, d_qkv, nh)
    if same:
        att_send, *mid_received = ordered(att_send, *mid_received)
        att = Whole(att_keep, att_send, groups)
        mid.add(mid_received)
        d_qkv, *terms = ordered(d_qkv, *mid.last_sends(), *att.terms)
        att.terms = terms[-2:]
        mid_received = mid.last_receive(terms[:-2])
        d_qkv, *sends = ordered(d_qkv, *att.sends())
        att_received = att.receive(sends)
    grad_input, sums = input_grad(d_qkv, x, grad_middle, attend_low, vec, mid_sums)
    if same:
        sums, *terms = ordered(sums, *att_received, *mid_received)
        att.terms = att.terms + terms[:3]
        att_received = att.last_receive(att.last_sends())
        red_grad, found = red.finish(red_received), mid.finish(terms[3:])
        per = 2 * own
        mid = jnp.concatenate(
            [found[:per], found[per + 32 :], found[per : per + own]], axis=0
        )
    else:
        red_parts = for_devices(
            red_keep, red_send, lambda parts: parts.reshape(count, own_red, model)
        )
        mid_parts = for_devices(mid_keep, mid_send, split_mid)
        att_parts = for_devices(
            [att_keep], [att_send], lambda parts: join_parts(parts, nh).reshape(count, own_in, flat)
        )
        red_grad, mid = scatter(*red_parts, groups), scatter(*mid_parts, groups)
        att_grad = scatter(*att_parts, groups)
    out_grad = mid[4 * own : 5 * own]
    exp_both = mid[: 4 * own].reshape(2, 2, own, model)
    kept = jnp.where(core == 0, exp_both[:, 0], exp_both[:, 1])
    beside = swap(jnp.where(core == 0, exp_both[:, 1], exp_both[:, 0]), 1)
    exp_grad = jnp.stack(
        [jnp.where(core == 0, kept, beside), jnp.where(core == 0, beside, kept)]
    ).reshape(wide, own, model)
    exp_grad = exp_grad.transpose(1, 0, 2).reshape(own, hidden)


    sums = all_sum(sums, groups[:2])
    if same:
        sums, *att_received = ordered(sums, *att_received)
    vector_grad = all_sum(sums, groups[2:])
    late_weights = (output_weight, expand_weight, reduce_weight)
    late_states = [
        (grad, first, second, weight)
        for grad, first, second, weight in zip(
            (out_grad, exp_grad, red_grad),
            (first_output, first_expand, first_reduce),
            (second_output, second_expand, second_reduce),
            late_weights,
        )
    ]
    late_found, late_sums = adapt(late_states, [1, 2, 3])
    if same:
        late_sums, *att_received = ordered(late_sums, *att_received)
        att_grad = att.finish(att_received)

    def planes(state):
        return state.transpose(1, 0, 2)

    vector_grad = lax.dynamic_slice_in_dim(vector_grad, place * own, own, 1)
    found, sums = adapt(
        [
            (att_grad, planes(first_attend), planes(second_attend), planes(attend_weight)),
            (vector_grad, first_vectors.T, second_vectors.T, vectors.T),
        ],
        [0, 4],
        late_sums,
    )
    sums = all_sum(sums, groups)
    adapted = [list(found[0]), *late_found, [a.T for a in found[1]]]
    *masters, trust_norms = master(
        sums,
        [found[0][2], *[a[2] for a in late_found], found[1][2]],
        [planes(attend_weight), *late_weights, vectors.T],
    )
    masters[4] = masters[4].T
    adapted[0] = [planes(a) for a in adapted[0]]
    masters[0] = planes(masters[0])
    return (
        hidden_states.reshape(rows, length, model),
        grad_input.reshape(rows, length, model),
        *[a[0] for a in adapted],
        *[a[1] for a in adapted],
        *masters,
        trust_norms,
    )


def solution(mesh):
    rows = P(AXES, None, None)
    state = [P("batch", None, "head")] + [P(AXES, None)] * 4
    return jax.shard_map(
        shards,
        mesh=mesh,
        in_specs=(rows, rows, P("batch", None), P("batch", None), P(AXES, None), *state * 3),
        out_specs=(rows, rows, *state * 3, P()),
        check_vma=False,
    )
```

time: 1890 us -> 404 us (0.21)
  matrix products: 563 us -> 0 us
  waiting for transfers between devices: 554 us -> 76.2 us
  local copies, waits for them, and re-layouts: 327 us -> 10.1 us
  Pallas kernels: 0 us -> 215 us
  blocking collectives: 160 us -> 0 us
  other arithmetic: 179 us -> 34.5 us
  loops' own time: 55.1 us -> 0 us
  starting transfers between devices: 18.1 us -> 50.4 us
    dot_general x136 -> x0, matrix products: 563 us -> none  [the longest x32 94.6 us: block_scores(): jnp.einsum('qhd,khd->hqk', query_block, key_rows, preferred_element_type=...]
    reduce_scatter x6 -> x0, waiting for transfers between devices: 449 us -> none  [the longest x2 194 us: shards(): lax.psum_scatter(grad_terms, 'head', scatter_dimension=0, tiled=True)]
    pallas_call x0 -> x13, Pallas kernels: none -> 215 us  [the longest x1 39.9 us: mlp_forward(): pl.pallas_call(mlp_forward_kernel, grid=(tokens // tile,), in_specs=Late....]
    reduce_sum x43 -> x1, other arithmetic: 81.2 us -> 0.13 us  [row_facts(): passes = jnp.sum(jnp.where(inside, counts[:, None, :], 0), axis=-1)]
    all_gather x2 -> x0, blocking collectives: 79.3 us -> none  [the longest x1 43.5 us: fetch(): lax.all_gather(vectors.astype(jnp.bfloat16), ('batch', 'head'), axis=0, t...]
    squeeze x56 -> x0, local copies, waits for them, and re-layouts: 79.1 us -> none  [the longest x48 68.4 us: shards(): lax.map(lambda parts: attend_forward(*parts), (query, key_rows, value_row...]
    all_gather x5 -> x1, waiting for transfers between devices: 90.9 us -> 12.9 us  [shards(): late_all = lax.all_gather(piece, AXES, axis=0, tiled=False)]
    ppermute x0 -> x48, waiting for transfers between devices: none -> 63.3 us  [swap(): return lax.ppermute(value, AXES, [(i, i ^ mask) for i in range(count)])]
  transfers between devices with their start and end apart: 15 -> 49, of which waited for: 7 -> 21; matrix products, arithmetic and copies ran while one was open for 45% -> 5% of each run, Pallas kernels for 0% -> 37%
where the time goes in v1:
time: 404 us; the launch traced here: 401 us
  Pallas kernels  215 us (53%)
  waiting for transfers between devices  76.2 us (19%)
  starting transfers between devices  50.4 us (12%)
  other arithmetic  34.5 us (9%)
  between operations  14.9 us (4%)
  local copies, waits for them, and re-layouts  10.1 us (2%)
    ppermute x48, waiting for transfers between devices, swap(): return lax.ppermute(value, AXES, [(i, i ^ mask) for i in range(count)])  63.3 us
    ppermute x48, starting transfers between devices, swap(): return lax.ppermute(value, AXES, [(i, i ^ mask) for i in range(count)])  50.4 us
    pallas_call x1, Pallas kernels, mlp_forward(): pl.pallas_call(mlp_forward_kernel, grid=(tokens // tile,), in_specs=Late....  39.9 us
    pallas_call x1, Pallas kernels, mlp_backward(): pl.pallas_call(mlp_backward_kernel, grid=(tokens // tile,), in_specs=Late...  36.1 us
    pallas_call x2, Pallas kernels, attend_backward(): pl.pallas_call(kernel, grid=(high - low,), in_specs=in_specs, out_specs=p...  29.8 us
    pallas_call x1, Pallas kernels, mid_weight_grad(): pl.pallas_call(mid_weight_grad_kernel, grid=(5,), in_specs=[SCALARS, whol...  21.5 us
    pallas_call x1, Pallas kernels, attend_forward(): pl.pallas_call(kernel, grid=(rows * pairs,), in_specs=[start_spec] + qkv_...  17.6 us
    pallas_call x1, Pallas kernels, reduce_weight_grad(): pl.pallas_call(reduce_weight_grad_kernel, grid=(hidden // model,), in_spe...  16.9 us
  transfers between devices with their start and end apart: 49, of which 21 were waited for; matrix products, arithmetic and copies ran while one was open for 5% of the time, Pallas kernels for 37%

profile of v1, /device:TPU:0, one launch (start us, length us, event | category | flops | bytes accessed | tf_op | source)
XLA Modules:
  0.0 401.3 jit_solution(5334878390816071946)
XLA Ops:
  12.3 2.7 collective-permute-start.1
  14.9 2.6 collective-permute-start.2
  17.5 4.4 %collective-permute-done.1 = bf16[1,112,576]{2,1,0:T(8,128)(2,1)S(1)} collective-permute-done((bf16[1,112,576]{2,1,0:T(8,128)(2,1)S(1)}, bf16[1,112,576]{2,1,0:T(8,128)(2,1)S(1)}, u32[]{:S(2)}, u32[]{:S(2)}) %collective-permute-start.1) | collective-permute-done | bytes 129056 | tf_op jit(solution)/shard_map/ppermute | solution.py:744
  21.9 8.6 %collective-permute-done.2 = bf16[1,112,576]{2,1,0:T(8,128)(2,1)S(1)} collective-permute-done((bf16[1,112,576]{2,1,0:T(8,128)(2,1)S(1)}, bf16[1,112,576]{2,1,0:T(8,128)(2,1)S(1)}, u32[]{:S(2)}, u32[]{:S(2)}) %collective-permute-start.2) | collective-permute-done | bytes 129056 | tf_op jit(solution)/shard_map/ppermute | solution.py:744
  34.4 11.3 %collective-permute-done.4 = bf16[4,112,576]{2,1,0:T(8,128)(2,1)S(1)} collective-permute-done((bf16[4,112,576]{2,1,0:T(8,128)(2,1)S(1)}, bf16[4,112,576]{2,1,0:T(8,128)(2,1)S(1)}, u32[]{:S(2)}, u32[]{:S(2)}) %collective-permute-start.4) | collective-permute-done | bytes 516128 | tf_op jit(solution)/shard_map/ppermute | solution.py:744
  45.8 4.6 %collective-permute-done.5 = bf16[4,112,576]{2,1,0:T(8,128)(2,1)S(1)} collective-permute-done((bf16[4,112,576]{2,1,0:T(8,128)(2,1)S(1)}, bf16[4,112,576]{2,1,0:T(8,128)(2,1)S(1)}, u32[]{:S(2)}, u32[]{:S(2)}) %collective-permute-start.5) | collective-permute-done | bytes 516128 | tf_op jit(solution)/shard_map/ppermute | solution.py:744
  50.6 15.2 %collective-permute-done.6 = bf16[4,112,576]{2,1,0:T(8,128)(2,1)S(1)} collective-permute-done((bf16[4,112,576]{2,1,0:T(8,128)(2,1)S(1)}, bf16[4,112,576]{2,1,0:T(8,128)(2,1)S(1)}, u32[]{:S(2)}, u32[]{:S(2)}) %collective-permute-start.6) | collective-permute-done | bytes 516128 | tf_op jit(solution)/shard_map/ppermute | solution.py:744
  70.5 15.0 %project.1 = (bf16[2048,768]{1,0:T(8,128)(2,1)}, bf16[2048,2304]{1,0:T(8,128)(2,1)}, bf16[768,2304]{1,0:T(8,128)(2,1)}, f32[12,768]{1,0:T(8,128)}) custom-call(s32[1]{0:T(128)} %bitcast.5.refs_0_.place_ref, bf16[2048,768]{1,0:T(8,128)(2,1)} %bitcast.118, bf16[16,112,576]{2,1,0:T(8,128)(2,1)} %copy-done.16, bf16[16,112,576]{2,1,0:T(8,128)(2,1)} %collective-permute-done.7.refs_3_), custom_call_target="tpu_custom_call" | custom-call | flops 4060000000 | bytes 262144 | tf_op jit(solution)/shard_map/project/pallas_call | solution.py:328
  85.6 17.6 %attend_forward.1 = (bf16[2048,768]{1,0:T(8,128)(2,1)}, f32[2,6,2,1024]{3,2,1,0:T(2,128)}) custom-call(s32[2,1,1024]{2,1,0:T(1,128)} %reshape.250.refs_0_, bf16[2048,2304]{1,0:T(8,128)(2,1)} %get-tuple-element.139.refs_1_.refs_2_.refs_3_, bf16[2048,2304]{1,0:T(8,128)(2,1)} %get-tuple-element.139.refs_1_.refs_2_.refs_3_, ...), custom_call_target="tpu_custom_call" | custom-call | flops 5219999744 | bytes 262144 | tf_op jit(solution)/shard_map/attend_forward/pallas_call | solution.py:213
  103.2 12.9 %all-gather.3.cloned.1.call-done = bf16[7168,768]{1,0:T(8,128)(2,1)} async-done(((bf16[224,768]{1,0:T(8,128)(2,1)}), bf16[7168,768]{1,0:T(8,128)(2,1)}) %all-gather.3.cloned.1.call-update) | async-done | bytes 11010064 | tf_op jit(solution)/shard_map/all_gather | solution.py:1041
  116.1 39.9 %mlp_forward.1 = (bf16[2048,768]{1,0:T(8,128)(2,1)}, f32[2048,768]{1,0:T(8,128)}, bf16[2048,768]{1,0:T(8,128)(2,1)}, bf16[2048,3072]{1,0:T(8,128)(2,1)}, bf16[20...) custom-call(bf16[32,224,768]{2,1,0:T(8,128)(2,1)} %bitcast.137, ...), custom_call_target="tpu_custom_call" | custom-call | flops 11600000000 | bytes 262144 | tf_op jit(solution)/shard_map/mlp_forward/pallas_call | solution.py:445
  156.0 16.9 %reduce_weight_grad.1 = (bf16[16,48,768]{2,1,0:T(8,128)(2,1)}, bf16[16,48,768]{2,1,0:T(8,128)(2,1)}, bf16[16,48,768]{2,1,0:T(8,128)(2,1)}, bf16[16,48,768]{2,1,0:T(8,128)(2,1)}) custom-call(s32[1]{0:T(128)} %bitcast.5.refs_0_.place_ref, bf16[2048,3072]{1,0:T(8,128)(2,1)} %get-tuple-element.143.a_ref, bf16[2048,768]{1,0:T(8,128)(2,1)} %get-tuple-element.144.b_ref), custom_call_target="tpu_custom_call" | custom-call | flops 4350000128 | bytes 262144 | tf_op jit(solution)/shard_map/reduce_weight_grad/pallas_call | solution.py:566
  173.4 36.1 %mlp_backward.1 = (bf16[2048,3072]{1,0:T(8,128)(2,1)}, f32[2048,768]{1,0:T(8,128)}, bf16[2048,768]{1,0:T(8,128)(2,1)}, bf16[2048,768]{1,0:T(8,128)(2,1)}, f32[8,768]{1,0:T(8,128)}) custom-call(bf16[32,224,768]{2,1,0:T(8,128)(2,1)} %bitcast.138, bf16[2048,768]{1,0:T(8,128)(2,1)} %bitcast.140, f32[2048,1]{1,0:T(8,128)} %bitcast.128, ...), custom_call_target="tpu_custom_call" | custom-call | flops 10439999488 | bytes 262144 | tf_op jit(solution)/shard_map/mlp_backward/pallas_call | solution.py:503
  213.8 21.5 %mid_weight_grad.1 = (bf16[16,80,768]{2,1,0:T(8,128)(2,1)}, bf16[16,48,768]{2,1,0:T(8,128)(2,1)}, bf16[16,80,768]{2,1,0:T(8,128)(2,1)}, bf16[16,48,768]{2,1,0:T(8,128)(2,1)}) custom-call(s32[1]{0:T(128)} %bitcast.5.refs_0_.place_ref, bf16[2048,768]{1,0:T(8,128)(2,1)} %get-tuple-element.151.nm_ref, bf16[2048,3072]{1,0:T(8,128)(2,1)} %get-tuple-element.162.gpre_ref, ...), custom_call_target="tpu_custom_call" | custom-call | flops 5510000128 | bytes 262144 | tf_op jit(solution)/shard_map/mid_weight_grad/pallas_call | solution.py:625
  241.9 8.7 %attend_backward.2.refs_7_ = bf16[3,2048,768]{2,1,0:T(8,128)(2,1)} custom-call(s32[2,1,1024]{2,1,0:T(1,128)} %reshape.250.refs_0_, bf16[2048,2304]{1,0:T(8,128)(2,1)} %get-tuple-element.139.refs_1_.refs_2_.refs_3_, bf16[2048,2304]{1,0:T(8,128)(2,1)} %get-tuple-element.139.refs_1_.refs_2_.refs_3_, ...), custom_call_target="tpu_custom_call" | custom-call | flops 2000999936 | bytes 262144 | tf_op jit(solution)/shard_map/attend_backward/pallas_call | solution.py:245
  253.2 2.3 add_bitcast_fusion.1
  257.5 2.1 add_convert_fusion.1
  265.1 2.1 collective-permute-start.20
  267.2 21.1 %attend_backward.3.refs_2_.d_ref = bf16[3,2048,768]{2,1,0:T(8,128)(2,1)} custom-call(s32[2,1,1024]{2,1,0:T(1,128)} %reshape.250.refs_0_, bf16[2048,2304]{1,0:T(8,128)(2,1)} %get-tuple-element.139.refs_1_.refs_2_.refs_3_, bf16[2048,2304]{1,0:T(8,128)(2,1)} %get-tuple-element.139.refs_1_.refs_2_.refs_3_, ...), custom_call_target="tpu_custom_call", output_to_operand_aliasing={{}: (7, {})} | custom-call | flops 6002999808 | bytes 262144 | tf_op jit(solution)/shard_map/attend_backward/pallas_call | solution.py:245
  290.3 2.0 add_convert_fusion.7
  294.4 13.7 %attend_weight_grad.1 = (bf16[16,96,576]{2,1,0:T(8,128)(2,1)}, bf16[16,96,576]{2,1,0:T(8,128)(2,1)}) custom-call(s32[1]{0:T(128)} %bitcast.5.refs_0_.place_ref, bf16[2048,768]{1,0:T(8,128)(2,1)} %get-tuple-element.196.refs_1_, bf16[3,2048,768]{2,1,0:T(8,128)(2,1)} %attend_backward.3.refs_2_.d_ref), custom_call_target="tpu_custom_call" | custom-call | flops 3769999872 | bytes 262144 | tf_op jit(solution)/shard_map/attend_weight_grad/pallas_call | solution.py:670
  308.2 2.1 add_bitcast_fusion.3
  310.3 2.3 add_bitcast_fusion
  322.7 16.1 %input_grad.1 = (bf16[2048,768]{1,0:T(8,128)(2,1)}, f32[12,768]{1,0:T(8,128)}) custom-call(bf16[3,2048,768]{2,1,0:T(8,128)(2,1)} %attend_backward.3.refs_2_.d_ref, bf16[2048,768]{1,0:T(8,128)(2,1)} %bitcast.120, f32[2048,768]{1,0:T(8,128)} %get-tuple-element.208.gm_ref, bf16[768,2304]{1,0:T(8,128)(2,1)} %get-tuple-element.209.w_ref, ...), custom_call_target="tpu_custom_call" | custom-call | flops 4640000000 | bytes 262144 | tf_op jit(solution)/shard_map/input_grad/pallas_call | solution.py:704
  349.2 2.1 collective-permute-start.37
  352.2 3.8 collective-permute-done.37
  366.7 3.4 adapt.2
  372.0 2.5 adapt.3
  383.3 2.3 collective-permute-start.46
  385.5 2.1 collective-permute-start.47
  388.0 3.1 collective-permute-done.47
  391.7 2.5 master.1
  (188 shorter events, 82.6 us)
Async XLA Ops:
  7.2 108.9 %all-gather.3.cloned.1.call-start = ((), (), s32[]{:S(2)}) async-start(), calls=%async_computation | async-start | bytes 11354112 | tf_op jit(solution)/shard_map/all_gather | solution.py:1041
  12.3 9.7 %collective-permute-start.1 = (bf16[1,112,576]{2,1,0:T(8,128)(2,1)S(1)}, bf16[1,112,576]{2,1,0:T(8,128)(2,1)S(1)}, u32[]{:S(2)}, u32[]{:S(2)}) collective-permute-start(bf16[1,112,576]{2,1,0:T(8,128)(2,1)S(1)} %fusion.9), channel_id=1, source_target_pairs={{0,8},{1,9},{2,10},{3,11},{4,12},{5,13},{6,14},{7,15},{8,0},{9,1},... | collective-permute-start | bytes 387080 | tf_op jit(solution)/shard_map/ppermute | solution.py:744
  14.9 15.7 %collective-permute-start.2 = (bf16[1,112,576]{2,1,0:T(8,128)(2,1)S(1)}, bf16[1,112,576]{2,1,0:T(8,128)(2,1)S(1)}, u32[]{:S(2)}, u32[]{:S(2)}) collective-permute-start(bf16[1,112,576]{2,1,0:T(8,128)(2,1)S(1)} %fusion.9), channel_id=1, source_target_pairs={{0,16},{1,17},{2,18},{3,19},{4,20},{5,21},{6,22},{7,23},{8,24},{9,... | collective-permute-start | bytes 387080 | tf_op jit(solution)/shard_map/ppermute | solution.py:744
  17.5 13.1 %collective-permute-start.3 = (bf16[1,112,576]{2,1,0:T(8,128)(2,1)S(1)}, bf16[1,112,576]{2,1,0:T(8,128)(2,1)S(1)}, u32[]{:S(2)}, u32[]{:S(2)}) collective-permute-start(bf16[1,112,576]{2,1,0:T(8,128)(2,1)S(1)} %fusion.9), channel_id=1, source_target_pairs={{0,24},{1,25},{2,26},{3,27},{4,28},{5,29},{6,30},{7,31},{8,16},{9,... | collective-permute-start | bytes 387080 | tf_op jit(solution)/shard_map/ppermute | solution.py:744
  30.7 15.1 %collective-permute-start.4 = (bf16[4,112,576]{2,1,0:T(8,128)(2,1)S(1)}, bf16[4,112,576]{2,1,0:T(8,128)(2,1)S(1)}, u32[]{:S(2)}, u32[]{:S(2)}) collective-permute-start(bf16[4,112,576]{2,1,0:T(8,128)(2,1)S(1)} %pad_maximum_fusion), channel_id=1, source_target_pairs={{0,2},{1,3},{2,0},{3,1},{4,6},{5,7},{6,4},{7,5},{8,10},{9,11},{10,... | collective-permute-start | bytes 1548296 | tf_op jit(solution)/shard_map/ppermute | solution.py:744
  32.3 18.2 %collective-permute-start.5 = (bf16[4,112,576]{2,1,0:T(8,128)(2,1)S(1)}, bf16[4,112,576]{2,1,0:T(8,128)(2,1)S(1)}, u32[]{:S(2)}, u32[]{:S(2)}) collective-permute-start(bf16[4,112,576]{2,1,0:T(8,128)(2,1)S(1)} %pad_maximum_fusion), channel_id=1, source_target_pairs={{0,4},{1,5},{2,6},{3,7},{4,0},{5,1},{6,2},{7,3},{8,12},{9,13},{10,... | collective-permute-start | bytes 1548296 | tf_op jit(solution)/shard_map/ppermute | solution.py:744
  33.9 31.8 %collective-permute-start.6 = (bf16[4,112,576]{2,1,0:T(8,128)(2,1)S(1)}, bf16[4,112,576]{2,1,0:T(8,128)(2,1)S(1)}, u32[]{:S(2)}, u32[]{:S(2)}) collective-permute-start(bf16[4,112,576]{2,1,0:T(8,128)(2,1)S(1)} %pad_maximum_fusion), channel_id=1, source_target_pairs={{0,6},{1,7},{2,4},{3,5},{4,2},{5,3},{6,0},{7,1},{8,14},{9,15},{10,... | collective-permute-start | bytes 1548296 | tf_op jit(solution)/shard_map/ppermute | solution.py:744
  172.9 36.6 %collective-permute-start.8 = (bf16[16,48,768]{2,1,0:T(8,128)(2,1)}, bf16[16,48,768]{2,1,0:T(8,128)(2,1)S(1)}, u32[]{:S(2)}, u32[]{:S(2)}) collective-permute-start(bf16[16,48,768]{2,1,0:T(8,128)(2,1)} %get-tuple-element.154), channel_id=1, source_target_pairs={{0,1},{1,0},{2,3},{3,2},{4,5},{5,4},{6,7},{7,6},{8,9},{9,8},{10,11... | collective-permute-start | bytes 3538952 | tf_op jit(solution)/shard_map/ppermute | solution.py:744
  173.2 36.3 %collective-permute-start.9 = (bf16[16,48,768]{2,1,0:T(8,128)(2,1)}, bf16[16,48,768]{2,1,0:T(8,128)(2,1)S(1)}, u32[]{:S(2)}, u32[]{:S(2)}) collective-permute-start(bf16[16,48,768]{2,1,0:T(8,128)(2,1)} %get-tuple-element.156), channel_id=1, source_target_pairs={{0,1},{1,0},{2,3},{3,2},{4,5},{5,4},{6,7},{7,6},{8,9},{9,8},{10,11... | collective-permute-start | bytes 3538952 | tf_op jit(solution)/shard_map/ppermute | solution.py:744
  211.7 23.7 %collective-permute-start.10 = (bf16[8,48,768]{2,1,0:T(8,128)(2,1)S(1)}, bf16[8,48,768]{2,1,0:T(8,128)(2,1)}, u32[]{:S(2)}, u32[]{:S(2)}) collective-permute-start(bf16[8,48,768]{2,1,0:T(8,128)(2,1)S(1)} %add_convert_fusion.3), channel_id=1, source_target_pairs={{0,4},{1,5},{2,6},{3,7},{4,0},{5,1},{6,2},{7,3},{8,12},{9,13},{10,... | collective-permute-start | bytes 1769480 | tf_op jit(solution)/shard_map/ppermute | solution.py:744
  213.2 22.2 %collective-permute-start.11 = (bf16[8,48,768]{2,1,0:T(8,128)(2,1)S(1)}, bf16[8,48,768]{2,1,0:T(8,128)(2,1)S(1)}, u32[]{:S(2)}, u32[]{:S(2)}) collective-permute-start(bf16[8,48,768]{2,1,0:T(8,128)(2,1)S(1)} %add_convert_fusion.2), channel_id=1, source_target_pairs={{0,2},{1,3},{2,0},{3,1},{4,6},{5,7},{6,4},{7,5},{8,10},{9,11},{10,... | collective-permute-start | bytes 1769480 | tf_op jit(solution)/shard_map/ppermute | solution.py:744
  236.2 14.5 %collective-permute-start.12 = (bf16[16,80,768]{2,1,0:T(8,128)(2,1)}, bf16[16,80,768]{2,1,0:T(8,128)(2,1)S(1)}, u32[]{:S(2)}, u32[]{:S(2)}) collective-permute-start(bf16[16,80,768]{2,1,0:T(8,128)(2,1)} %get-tuple-element.174), channel_id=1, source_target_pairs={{0,1},{1,0},{2,3},{3,2},{4,5},{5,4},{6,7},{7,6},{8,9},{9,8},{10,11... | collective-permute-start | bytes 5898248 | tf_op jit(solution)/shard_map/ppermute | solution.py:744
  236.2 14.5 %collective-permute-start.13 = (bf16[16,48,768]{2,1,0:T(8,128)(2,1)}, bf16[16,48,768]{2,1,0:T(8,128)(2,1)S(1)}, u32[]{:S(2)}, u32[]{:S(2)}) collective-permute-start(bf16[16,48,768]{2,1,0:T(8,128)(2,1)} %get-tuple-element.176), channel_id=1, source_target_pairs={{0,1},{1,0},{2,3},{3,2},{4,5},{5,4},{6,7},{7,6},{8,9},{9,8},{10,11... | collective-permute-start | bytes 3538952 | tf_op jit(solution)/shard_map/ppermute | solution.py:744
  239.9 10.7 %collective-permute-start.14 = (bf16[4,48,768]{2,1,0:T(8,128)(2,1)}, bf16[4,48,768]{2,1,0:T(8,128)(2,1)S(1)}, u32[]{:S(2)}, u32[]{:S(2)}) collective-permute-start(bf16[4,48,768]{2,1,0:T(8,128)(2,1)} %add_convert_fusion.10), channel_id=1, source_target_pairs={{0,2},{1,3},{2,0},{3,1},{4,6},{5,7},{6,4},{7,5},{8,10},{9,11},{10,... | collective-permute-start | bytes 884744 | tf_op jit(solution)/shard_map/ppermute | solution.py:744
  241.3 9.3 %collective-permute-start.15 = (bf16[4,48,768]{2,1,0:T(8,128)(2,1)S(1)}, bf16[4,48,768]{2,1,0:T(8,128)(2,1)S(1)}, u32[]{:S(2)}, u32[]{:S(2)}) collective-permute-start(bf16[4,48,768]{2,1,0:T(8,128)(2,1)S(1)} %add_convert_fusion.9), channel_id=1, source_target_pairs={{0,4},{1,5},{2,6},{3,7},{4,0},{5,1},{6,2},{7,3},{8,12},{9,13},{10,... | collective-permute-start | bytes 884744 | tf_op jit(solution)/shard_map/ppermute | solution.py:744
  260.8 27.6 %collective-permute-start.16 = (bf16[8,80,768]{2,1,0:T(8,128)(2,1)}, bf16[8,80,768]{2,1,0:T(8,128)(2,1)}, u32[]{:S(2)}, u32[]{:S(2)}) collective-permute-start(bf16[8,80,768]{2,1,0:T(8,128)(2,1)} %add_convert_fusion), channel_id=1, source_target_pairs={{0,4},{1,5},{2,6},{3,7},{4,0},{5,1},{6,2},{7,3},{8,12},{9,13},{10,... | collective-permute-start | bytes 2949128 | tf_op jit(solution)/shard_map/ppermute | solution.py:744
  262.2 26.1 %collective-permute-start.17 = (bf16[8,48,768]{2,1,0:T(8,128)(2,1)}, bf16[8,48,768]{2,1,0:T(8,128)(2,1)}, u32[]{:S(2)}, u32[]{:S(2)}) collective-permute-start(bf16[8,48,768]{2,1,0:T(8,128)(2,1)} %add_convert_fusion.1), channel_id=1, source_target_pairs={{0,2},{1,3},{2,0},{3,1},{4,6},{5,7},{6,4},{7,5},{8,10},{9,11},{10,... | collective-permute-start | bytes 1769480 | tf_op jit(solution)/shard_map/ppermute | solution.py:744
  262.8 25.5 %collective-permute-start.18 = (bf16[96,768]{1,0:T(8,128)(2,1)}, bf16[96,768]{1,0:T(8,128)(2,1)}, u32[]{:S(2)}, u32[]{:S(2)}) collective-permute-start(bf16[96,768]{1,0:T(8,128)(2,1)} %pad_maximum_fusion.7), channel_id=1, source_target_pairs={{0,8},{1,9},{2,10},{3,11},{4,12},{5,13},{6,14},{7,15},{8,0},{9,1},... | collective-permute-start | bytes 442376 | tf_op jit(solution)/shard_map/ppermute | solution.py:744
  264.1 24.3 %collective-permute-start.19 = (bf16[96,768]{1,0:T(8,128)(2,1)}, bf16[96,768]{1,0:T(8,128)(2,1)}, u32[]{:S(2)}, u32[]{:S(2)}) collective-permute-start(bf16[96,768]{1,0:T(8,128)(2,1)} %pad_maximum_fusion.8), channel_id=1, source_target_pairs={{0,16},{1,17},{2,18},{3,19},{4,20},{5,21},{6,22},{7,23},{8,24},{9,... | collective-permute-start | bytes 442376 | tf_op jit(solution)/shard_map/ppermute | solution.py:744
  265.1 23.2 %collective-permute-start.20 = (bf16[96,768]{1,0:T(8,128)(2,1)}, bf16[96,768]{1,0:T(8,128)(2,1)}, u32[]{:S(2)}, u32[]{:S(2)}) collective-permute-start(bf16[96,768]{1,0:T(8,128)(2,1)} %pad_maximum_fusion.9), channel_id=1, source_target_pairs={{0,24},{1,25},{2,26},{3,27},{4,28},{5,29},{6,30},{7,31},{8,16},{9,... | collective-permute-start | bytes 442376 | tf_op jit(solution)/shard_map/ppermute | solution.py:744
  292.4 15.8 %collective-permute-start.21 = (bf16[4,80,768]{2,1,0:T(8,128)(2,1)}, bf16[4,80,768]{2,1,0:T(8,128)(2,1)}, u32[]{:S(2)}, u32[]{:S(2)}) collective-permute-start(bf16[4,80,768]{2,1,0:T(8,128)(2,1)} %add_convert_fusion.7), channel_id=1, source_target_pairs={{0,2},{1,3},{2,0},{3,1},{4,6},{5,7},{6,4},{7,5},{8,10},{9,11},{10,... | collective-permute-start | bytes 1474568 | tf_op jit(solution)/shard_map/ppermute | solution.py:744
  293.8 14.3 %collective-permute-start.22 = (bf16[4,48,768]{2,1,0:T(8,128)(2,1)}, bf16[4,48,768]{2,1,0:T(8,128)(2,1)}, u32[]{:S(2)}, u32[]{:S(2)}) collective-permute-start(bf16[4,48,768]{2,1,0:T(8,128)(2,1)} %add_convert_fusion.8), channel_id=1, source_target_pairs={{0,4},{1,5},{2,6},{3,7},{4,0},{5,1},{6,2},{7,3},{8,12},{9,13},{10,... | collective-permute-start | bytes 884744 | tf_op jit(solution)/shard_map/ppermute | solution.py:744
  313.4 7.6 %collective-permute-start.27 = (bf16[128,768]{1,0:T(8,128)(2,1)}, bf16[128,768]{1,0:T(8,128)(2,1)}, u32[]{:S(2)}, u32[]{:S(2)}) collective-permute-start(bf16[128,768]{1,0:T(8,128)(2,1)} %pad_maximum_fusion.3), channel_id=1, source_target_pairs={{0,8},{1,9},{2,10},{3,11},{4,12},{5,13},{6,14},{7,15},{8,0},{9,1},... | collective-permute-start | bytes 589832 | tf_op jit(solution)/shard_map/ppermute | solution.py:744
  314.7 24.2 %collective-permute-start.24 = (bf16[4,96,576]{2,1,0:T(8,128)(2,1)S(1)}, bf16[4,96,576]{2,1,0:T(8,128)(2,1)S(1)}, u32[]{:S(2)}, u32[]{:S(2)}) collective-permute-start(bf16[4,96,576]{2,1,0:T(8,128)(2,1)S(1)} %get-tuple-element.213), channel_id=1, source_target_pairs={{0,2},{1,3},{2,0},{3,1},{4,6},{5,7},{6,4},{7,5},{8,10},{9,11},{10,... | collective-permute-start | bytes 1327112 | tf_op jit(solution)/shard_map/ppermute | solution.py:744
  316.2 22.7 %collective-permute-start.25 = (bf16[4,96,576]{2,1,0:T(8,128)(2,1)S(1)}, bf16[4,96,576]{2,1,0:T(8,128)(2,1)S(1)}, u32[]{:S(2)}, u32[]{:S(2)}) collective-permute-start(bf16[4,96,576]{2,1,0:T(8,128)(2,1)S(1)} %get-tuple-element.214), channel_id=1, source_target_pairs={{0,4},{1,5},{2,6},{3,7},{4,0},{5,1},{6,2},{7,3},{8,12},{9,13},{10,... | collective-permute-start | bytes 1327112 | tf_op jit(solution)/shard_map/ppermute | solution.py:744
  316.7 23.3 %collective-permute-start.26 = (bf16[4,96,576]{2,1,0:T(8,128)(2,1)S(1)}, bf16[4,96,576]{2,1,0:T(8,128)(2,1)S(1)}, u32[]{:S(2)}, u32[]{:S(2)}) collective-permute-start(bf16[4,96,576]{2,1,0:T(8,128)(2,1)S(1)} %get-tuple-element.215), channel_id=1, source_target_pairs={{0,6},{1,7},{2,4},{3,5},{4,2},{5,3},{6,0},{7,1},{8,14},{9,15},{10,... | collective-permute-start | bytes 1327112 | tf_op jit(solution)/shard_map/ppermute | solution.py:744
  318.2 20.7 %collective-permute-start.28 = (bf16[128,768]{1,0:T(8,128)(2,1)S(1)}, bf16[128,768]{1,0:T(8,128)(2,1)S(1)}, u32[]{:S(2)}, u32[]{:S(2)}) collective-permute-start(bf16[128,768]{1,0:T(8,128)(2,1)S(1)} %pad_maximum_fusion.4), channel_id=1, source_target_pairs={{0,16},{1,17},{2,18},{3,19},{4,20},{5,21},{6,22},{7,23},{8,24},{9,... | collective-permute-start | bytes 589832 | tf_op jit(solution)/shard_map/ppermute | solution.py:744
  321.0 17.8 %collective-permute-start.29 = (bf16[128,768]{1,0:T(8,128)(2,1)S(1)}, bf16[128,768]{1,0:T(8,128)(2,1)S(1)}, u32[]{:S(2)}, u32[]{:S(2)}) collective-permute-start(bf16[128,768]{1,0:T(8,128)(2,1)S(1)} %pad_maximum_fusion.5), channel_id=1, source_target_pairs={{0,24},{1,25},{2,26},{3,27},{4,28},{5,29},{6,30},{7,31},{8,16},{9,... | collective-permute-start | bytes 589832 | tf_op jit(solution)/shard_map/ppermute | solution.py:744
  341.5 10.7 %collective-permute-start.35 = (bf16[96,576]{1,0:T(8,128)(2,1)S(1)}, bf16[96,576]{1,0:T(8,128)(2,1)S(1)}, u32[]{:S(2)}, u32[]{:S(2)}) collective-permute-start(bf16[96,576]{1,0:T(8,128)(2,1)S(1)} %get-tuple-element.264), channel_id=1, source_target_pairs={{0,8},{1,9},{2,10},{3,11},{4,12},{5,13},{6,14},{7,15},{8,0},{9,1},... | collective-permute-start | bytes 331784 | tf_op jit(solution)/shard_map/ppermute | solution.py:744
  342.4 9.8 %collective-permute-start.36 = (bf16[96,576]{1,0:T(8,128)(2,1)S(1)}, bf16[96,576]{1,0:T(8,128)(2,1)S(1)}, u32[]{:S(2)}, u32[]{:S(2)}) collective-permute-start(bf16[96,576]{1,0:T(8,128)(2,1)S(1)} %get-tuple-element.263), channel_id=1, source_target_pairs={{0,16},{1,17},{2,18},{3,19},{4,20},{5,21},{6,22},{7,23},{8,24},{9,... | collective-permute-start | bytes 331784 | tf_op jit(solution)/shard_map/ppermute | solution.py:744
  351.3 13.9 %collective-permute-start.30 = (f32[2,24,768]{2,1,0:T(8,128)S(1)}, f32[2,24,768]{2,1,0:T(8,128)S(1)}, u32[]{:S(2)}, u32[]{:S(2)}) collective-permute-start(f32[2,24,768]{2,1,0:T(8,128)S(1)} %select_bitcast_fusion.2), channel_id=1, source_target_pairs={{0,1},{1,0},{2,3},{3,2},{4,5},{5,4},{6,7},{7,6},{8,9},{9,8},{10,11... | collective-permute-start | bytes 442376 | tf_op jit(solution)/shard_map/ppermute | solution.py:744
  356.0 6.9 %collective-permute-start.38 = (f32[12,768]{1,0:T(8,128)S(1)}, f32[12,768]{1,0:T(8,128)S(1)}, u32[]{:S(2)}, u32[]{:S(2)}) collective-permute-start(f32[12,768]{1,0:T(8,128)S(1)} %add_add_fusion), channel_id=1, source_target_pairs={{0,8},{1,9},{2,10},{3,11},{4,12},{5,13},{6,14},{7,15},{8,0},{9,1},... | collective-permute-start | bytes 110600 | tf_op jit(solution)/shard_map/ppermute | solution.py:744
  (36 other events, 263.4 us)
Sparse Core Ops, SparseCore 0:
  12.0 104.0 all-gather.2

commit v2 on v1

--- a/solution.py
+++ b/solution.py
@@ -104,7 +104,7 @@
         last(*both)
 
 
-def attend_forward_kernel(fresh, start_ref, q_ref, k_ref, v_ref, o_ref, log_ref, cap_ref):
+def attend_forward_kernel(fresh, start_ref, q_ref, k_ref, v_ref, o_ref, p_ref, cap_ref):
     length = q_ref.shape[0]
     pl.when(fresh)(lambda: fill_caps(start_ref, cap_ref, length))
     value_t = v_ref[...].T
@@ -115,32 +115,24 @@
         return dot(k_ref[first : first + count, :], query, NT)
 
     def soften(unit, scores):
-        number, (low, _, count) = unit
+        number, (_, _, count) = unit
         scores = jnp.minimum(scores, cap_of(cap_ref, number, count))
-        top = jnp.max(scores, axis=0, keepdims=True)
-        grown = jnp.exp(scores - top)
-        whole_sum = jnp.sum(grown, axis=0, keepdims=True)
-        logs = top + jnp.log(whole_sum)
-        log_ref[0, 0, :, low : low + BLOCK] = jnp.concatenate(
-            [logs[:, :BLOCK], logs[:, BLOCK:]], axis=0
-        )
-        return grown.astype(BF16), 1.0 / whole_sum
-
-    def mix(unit, found):
+        grown = jnp.exp(scores - jnp.max(scores, axis=0, keepdims=True))
+        probs = (grown * (1.0 / total(grown))).astype(BF16)
+        p_ref[0, 0, number, :count] = probs
+        return probs
+
+    def mix(unit, probs):
         _, (low, first, count) = unit
-        grown, scale = found
-        result = dot(value_t[:, first : first + count], grown) * scale
+        result = dot(value_t[:, first : first + count], probs)
         o_ref[low : low + BLOCK, :] = of_heads(result).T.astype(BF16)
 
     in_stages(list(enumerate(windows(length))), 4, 1, score, soften, mix)
 
 
-def attend_backward_kernel(
-    fresh, start_ref, q_ref, k_ref, v_ref, o_ref, do_ref, log_ref, *rest
-):
-    d_ref, cap_ref = rest[-2:]
+def attend_backward_kernel(q_ref, k_ref, v_ref, o_ref, do_ref, p_ref, *rest):
+    d_ref = rest[-1]
     length = q_ref.shape[0]
-    pl.when(fresh)(lambda: fill_caps(start_ref, cap_ref, length))
     key_t = k_ref[...].T
     grad_key, grad_value = {}, {}
 
@@ -150,23 +142,17 @@
     def grad_of(low):
         return for_heads(do_ref[low : low + BLOCK, :])
 
-    def side_by_side(values):
-        return jnp.concatenate(values, axis=1)
-
     def score(unit):
         _, (low, first, count) = unit
-        key, value = k_ref[first : first + count, :], v_ref[first : first + count, :]
-        return dot(key, query_of(low), NT), dot(value, grad_of(low), NT)
-
-    def soften(unit, found):
+        return dot(v_ref[first : first + count, :], grad_of(low), NT)
+
+    def soften(unit, grad_probs):
         number, (low, _, count) = unit
-        scores, grad_probs = found
         product = do_ref[low : low + BLOCK, :].astype(F32) * o_ref[low : low + BLOCK, :].astype(F32)
         product = product.T
-        inner = side_by_side([total(product[:HEAD_DIM]), total(product[HEAD_DIM:])])
-        logs = side_by_side([log_ref[0, 0, h : h + 1, low : low + BLOCK] for h in range(2)])
-        probs = jnp.exp(jnp.minimum(scores, cap_of(cap_ref, number, count)) - logs)
-        return probs.astype(BF16), (probs * (grad_probs - inner)).astype(BF16)
+        inner = jnp.concatenate([total(product[:HEAD_DIM]), total(product[HEAD_DIM:])], axis=1)
+        probs = p_ref[0, 0, number, :count]
+        return probs, (probs.astype(F32) * (grad_probs - inner)).astype(BF16)
 
     def mix(unit, found):
         _, (low, first, count) = unit
@@ -196,16 +182,20 @@
 
     qkv = [pl.BlockSpec((length, pair), columns(n)) for n in range(3)]
     rows = pl.BlockSpec((length, pair), columns(0))
-    logs = pl.BlockSpec((1, 1, 2, length), lambda i: (*at(i), 0, 0))
+    probs = pl.BlockSpec((1, 1) + probs_shape(length), lambda i: (*at(i), 0, 0, 0))
     start = pl.BlockSpec((1, 1, length), lambda i: (at(i)[0], 0, 0))
-    return start, qkv, rows, logs, lambda i: (0, *at(i))
+    return start, qkv, rows, probs, lambda i: (0, *at(i))
+
+
+def probs_shape(length):
+    return (length // BLOCK, SPAN + BLOCK, 2 * BLOCK)
 
 
 def attend_forward(start, qkv, length):
     tokens, model = qkv.shape[0], qkv.shape[1] // 3
     pairs = model // (2 * HEAD_DIM)
     rows = tokens // length
-    start_spec, qkv_specs, row_spec, log_spec, _ = attention_specs(length, pairs)
+    start_spec, qkv_specs, row_spec, probs_spec, _ = attention_specs(length, pairs)
 
     def kernel(*refs):
         attend_forward_kernel(pl.program_id(0) % pairs == 0, *refs)
@@ -214,10 +204,10 @@
         kernel,
         grid=(rows * pairs,),
         in_specs=[start_spec] + qkv_specs,
-        out_specs=[row_spec, log_spec],
+        out_specs=[row_spec, probs_spec],
         out_shape=[
             jax.ShapeDtypeStruct((tokens, model), BF16),
-            jax.ShapeDtypeStruct((rows, pairs, 2, length), F32),
+            jax.ShapeDtypeStruct((rows, pairs) + probs_shape(length), BF16),
         ],
         scratch_shapes=[pltpu.VMEM((length // BLOCK, SPAN + BLOCK, BLOCK), F32)],
         compiler_params=params(),
@@ -226,32 +216,26 @@
     )(start, qkv, qkv, qkv)
 
 
-def attend_backward(start, qkv, out, grad, logs, length, low, high, before=None):
+def attend_backward(qkv, out, grad, probs, length, low, high, before=None):
     tokens, model = out.shape
     pairs = model // (2 * HEAD_DIM)
-    start_spec, qkv_specs, row_spec, log_spec, at = attention_specs(length, pairs, low)
-    operands = [start, qkv, qkv, qkv, out, grad, logs]
-    in_specs = [start_spec] + qkv_specs + [row_spec, row_spec, log_spec]
+    _, qkv_specs, row_spec, probs_spec, at = attention_specs(length, pairs, low)
+    operands = [qkv, qkv, qkv, out, grad, probs]
+    in_specs = qkv_specs + [row_spec, row_spec, probs_spec]
     aliases = {}
     if before is not None:
         aliases = {len(operands): 0}
         operands.append(before)
         in_specs.append(pl.BlockSpec(memory_space=pl.ANY))
-
-    def kernel(*refs):
-        fresh = (pl.program_id(0) == 0) | ((pl.program_id(0) + low) % pairs == 0)
-        attend_backward_kernel(fresh, *refs)
-
     return pl.pallas_call(
-        kernel,
+        attend_backward_kernel,
         grid=(high - low,),
         in_specs=in_specs,
         out_specs=pl.BlockSpec((3, length, 2 * HEAD_DIM), at),
         out_shape=jax.ShapeDtypeStruct((3, tokens, model), BF16),
-        scratch_shapes=[pltpu.VMEM((length // BLOCK, SPAN + BLOCK, BLOCK), F32)],
         input_output_aliases=aliases,
         compiler_params=params(),
-        cost_estimate=cost(2.3 * (high - low)),
+        cost_estimate=cost(2.0 * (high - low)),
         name="attend_backward",
     )(*operands)
 
@@ -575,12 +559,22 @@
     return found[:2], found[2:]
 
 
-def mid_weight_grad_kernel(place_ref, nm_ref, gpre_ref, ctx_ref, ga_ref, *outs):
+def mid_weight_grad_kernel(place_ref, nm_ref, gpre_ref, ctx_hbm, ga_hbm, *outs):
+    *outs, ctx_ref, ga_ref, sems = outs
+    copies = [
+        pltpu.make_async_copy(ctx_hbm, ctx_ref, sems.at[0]),
+        pltpu.make_async_copy(ga_hbm, ga_ref, sems.at[1]),
+    ]
     slots, rows, model = outs[0].shape
     per = model // slots
     step = pl.program_id(0)
     last = pl.num_programs(0) - 1
     place = place_ref[0]
+
+    @pl.when(step == 1)
+    def _():
+        for copy in copies:
+            copy.start()
 
     for c in range(4):
 
@@ -599,6 +593,8 @@
 
     @pl.when(step == last)
     def _():
+        for copy in copies:
+            copy.wait()
         result = dot(ctx_ref[...], ga_ref[...], TN)
         half = per // 2
         empty = jnp.zeros((rows - per - half, model), F32)
@@ -629,10 +625,15 @@
             SCALARS,
             whole(nm.shape),
             pl.BlockSpec((tokens, model), lambda i: (0, jnp.minimum(i, 3))),
-            whole(ctx.shape),
-            whole(ga.shape),
+            pl.BlockSpec(memory_space=pl.ANY),
+            pl.BlockSpec(memory_space=pl.ANY),
         ],
         **outs_of(*shapes * 2),
+        scratch_shapes=[
+            pltpu.VMEM(ctx.shape, BF16),
+            pltpu.VMEM(ga.shape, BF16),
+            pltpu.SemaphoreType.DMA((2,)),
+        ],
         compiler_params=params(),
         cost_estimate=cost(19),
         name="mid_weight_grad",
@@ -678,7 +679,7 @@
     )(place, nl, d_qkv)
 
 
-def input_grad_kernel(d_ref, x_ref, gm_ref, w_ref, vec_ref, mid_ref, out_ref, sum_ref):
+def input_grad_kernel(d_ref, x_ref, gm_ref, w_ref, vec_ref, mid_ref, out_ref, sum_ref, part_ref):
     model = x_ref.shape[1]
 
     @pl.when(pl.program_id(0) == 0)
@@ -697,6 +698,14 @@
     sum_ref[3:4, :] += total(d_ref[2].astype(F32))
     out_ref[...] = (gm_ref[...] + norm_back(back * vec_ref[0:1, :], normed, factor)).astype(BF16)
 
+    @pl.when(pl.program_id(0) == pl.num_programs(0) - 1)
+    def _():
+        count = part_ref.shape[0]
+        each = model // count
+        part_ref[...] = jnp.zeros_like(part_ref)
+        for n in range(count):
+            part_ref[n, : sum_ref.shape[0], :each] = sum_ref[:, n * each : (n + 1) * each]
+
 
 def input_grad(d_qkv, x, gm, w, vec, mid_sums, tile=512):
     tokens, model = x.shape
@@ -708,9 +717,15 @@
             pl.BlockSpec((3, tile, model), lambda i: (0, i, 0)), row, row,
             whole(w.shape), whole(vec.shape), whole(mid_sums.shape),
         ],
-        out_specs=[row, pl.BlockSpec(vec.shape, lambda i: (0, 0))],
+        out_specs=[
+            row,
+            pl.BlockSpec(vec.shape, lambda i: (0, 0)),
+            pl.BlockSpec((PARTS, 16, 128), lambda i: (0, 0, 0)),
+        ],
         out_shape=[
-            jax.ShapeDtypeStruct((tokens, model), BF16), jax.ShapeDtypeStruct(vec.shape, F32),
+            jax.ShapeDtypeStruct((tokens, model), BF16),
+            jax.ShapeDtypeStruct(vec.shape, F32),
+            jax.ShapeDtypeStruct((PARTS, 16, 128), F32),
         ],
         compiler_params=params(),
         cost_estimate=cost(16),
@@ -876,10 +891,10 @@
     return [jnp.take(parts, place ^ (masks | bit), axis=0) for bit in range(2)]
 
 
-def adapt_kernel(rows, *refs):
+def adapt_kernel(rows, copies, *refs):
     count = len(rows)
     inputs, outputs = refs[: 4 * count + 1], refs[4 * count + 1 :]
-    sum_ref = outputs[-1]
+    sum_ref = outputs[3 * count]
     sum_ref[...] = inputs[-1][...]
     half = sum_ref.shape[0] // 2
     correct = 1.0 - BETA**STEP
@@ -887,11 +902,14 @@
         grad_ref, first_ref, second_ref, weight_ref = inputs[4 * number : 4 * number + 4]
         moment_ref, square_ref, update_ref = outputs[3 * number : 3 * number + 3]
         planes = weight_ref.shape[0] if len(weight_ref.shape) == 3 else 1
-        width = grad_ref.shape[1] // planes
+        width = weight_ref.shape[-1]
         norms = []
         for n in range(planes):
             at = n if len(weight_ref.shape) == 3 else Ellipsis
-            grad = grad_ref[:, n * width : (n + 1) * width]
+            if len(grad_ref.shape) == 3:
+                grad = jnp.sum(grad_ref[...], axis=0)[: weight_ref.shape[0], :width]
+            else:
+                grad = grad_ref[:, n * width : (n + 1) * width]
             moment = BETA * first_ref[at] + (1.0 - BETA) * grad
             square = BETA * second_ref[at] + (1.0 - BETA) * grad * grad
             weight = weight_ref[at]
@@ -906,15 +924,25 @@
                 norm = total(norm)
             place = n * half + row
             sum_ref[place : place + norm.shape[0], :] = jnp.broadcast_to(norm, (norm.shape[0], 128))
-
-
-def adapt(states, rows, sums=None):
+    if copies:
+        outputs[-1][...] = jnp.broadcast_to(diagonal(sum_ref[...]), outputs[-1].shape)
+
+
+def diagonal(values):
+    row = lax.broadcasted_iota(jnp.int32, values.shape, 0)
+    lane = lax.broadcasted_iota(jnp.int32, values.shape, 1)
+    return total(jnp.where(row == lane, values, 0.0))
+
+
+def adapt(states, rows, sums=None, copies=0):
     if sums is None:
         sums = jnp.zeros((32, 128), F32)
     operands = [array for state in states for array in state] + [sums]
     shapes = [state[3].shape for state in states for _ in range(3)] + [sums.shape]
-    *found, sums = pl.pallas_call(
-        lambda *refs: adapt_kernel(rows, *refs),
+    if copies:
+        shapes.append((copies, 8, 128))
+    found = pl.pallas_call(
+        lambda *refs: adapt_kernel(rows, copies, *refs),
         grid=(1,),
         in_specs=[whole(a.shape) for a in operands],
         out_specs=[pl.BlockSpec(s, lambda *_, n=len(s): (0,) * n) for s in shapes],
@@ -923,30 +951,38 @@
         cost_estimate=cost(4),
         name="adapt",
     )(*operands)
-    return [found[3 * n : 3 * n + 3] for n in range(len(states))], sums
+    return [found[3 * n : 3 * n + 3] for n in range(len(states))], found[-1]
 
 
 def master_kernel(sum_ref, *refs):
     *refs, trust_ref = refs
     count = len(refs) // 3
-    half = sum_ref.shape[0] // 2
-    norms = [jnp.sqrt(sum_ref[n * half : (n + 1) * half, :]) for n in range(2)]
+    width = trust_ref.shape[1]
+    if len(sum_ref.shape) == 3:
+        line = jnp.sum(sum_ref[...], axis=0)[:1]
+    else:
+        line = diagonal(sum_ref[...])
+    norms = [jnp.sqrt(line[:, n * width : (n + 1) * width]) for n in range(2)]
     ratio = norms[0] / (norms[1] + ADAM_EPS)
-    row = lax.broadcasted_iota(jnp.int32, ratio.shape, 0)
-    lane = lax.broadcasted_iota(jnp.int32, ratio.shape, 1)
     for n, value in enumerate([*norms, ratio]):
-        line = jnp.log(total(jnp.where(row == lane, value, 0.0)))
-        trust_ref[n : n + 1, :] = line[:, : trust_ref.shape[1]]
+        trust_ref[n : n + 1, :] = jnp.log(value)
     for n in range(count):
         update_ref, weight_ref, out_ref = refs[n], refs[count + n], refs[2 * count + n]
-        scale = RATE * (ratio[n : n + 1, :1] if n < 4 else ratio[4:, :1])
+        if n < 4:
+            scale = RATE * ratio[:, n : n + 1]
+        else:
+            shape = (weight_ref.shape[0], width)
+            row = lax.broadcasted_iota(jnp.int32, shape, 0)
+            lane = lax.broadcasted_iota(jnp.int32, shape, 1)
+            picked = jnp.where(lane == row + 4, jnp.broadcast_to(ratio, shape), 0.0)
+            scale = RATE * jnp.sum(picked, axis=1, keepdims=True)
         for at in range(weight_ref.shape[0]) if len(weight_ref.shape) == 3 else [Ellipsis]:
             out_ref[at] = weight_ref[at] - scale * update_ref[at]
 
 
-def master(sums, updates, weights):
+def master(sums, updates, weights, width):
     arrays = [sums, *updates, *weights]
-    shapes = [a.shape for a in weights] + [(3, sums.shape[0] // 2)]
+    shapes = [a.shape for a in weights] + [(3, width)]
     return pl.pallas_call(
         master_kernel,
         grid=(1,),
@@ -1064,7 +1100,7 @@
     normed_low, qkv, attend_low, vec = project(
         kernel_place, x, attend_own, attend_other, nh, cols
     )
-    context, logs = attend_forward(start_of, qkv, length)
+    context, probs = attend_forward(start_of, qkv, length)
     if not same:
         late = late_all
         both, per = 2 * own, 2 * model // PARTS
@@ -1130,7 +1166,7 @@
         red_received = red.receive(sends)
 
     pairs = model // (2 * HEAD_DIM)
-    operands = (start_of, qkv, context, grad_context, logs, length)
+    operands = (qkv, context, grad_context, probs, length)
     d_qkv = attend_backward(*operands, 0, pairs // 2)
     if same:
         d_qkv, *terms = ordered(d_qkv, *mid.flat(), *red_received)
@@ -1156,9 +1192,9 @@
         mid_received = mid.last_receive(terms[:-2])
         d_qkv, *sends = ordered(d_qkv, *att.sends())
         att_received = att.receive(sends)
-    grad_input, sums = input_grad(d_qkv, x, grad_middle, attend_low, vec, mid_sums)
+    grad_input, sums, sum_parts = input_grad(d_qkv, x, grad_middle, attend_low, vec, mid_sums)
     if same:
-        sums, *terms = ordered(sums, *att_received, *mid_received)
+        sum_parts, *terms = ordered(sum_parts, *att_received, *mid_received)
         att.terms = att.terms + terms[:3]
         att_received = att.last_receive(att.last_sends())
         red_grad, found = red.finish(red_received), mid.finish(terms[3:])
@@ -1186,10 +1222,10 @@
     exp_grad = exp_grad.transpose(1, 0, 2).reshape(own, hidden)
 
 
-    sums = all_sum(sums, groups[:2])
     if same:
-        sums, *att_received = ordered(sums, *att_received)
-    vector_grad = all_sum(sums, groups[2:])
+        vector_grad = lax.all_to_all(sum_parts, AXES, 0, 0, tiled=True)
+    else:
+        vector_grad = lax.dynamic_slice_in_dim(all_sum(sums, groups), place * own, own, 1)
     late_weights = (output_weight, expand_weight, reduce_weight)
     late_states = [
         (grad, first, second, weight)
@@ -1208,7 +1244,6 @@
     def planes(state):
         return state.transpose(1, 0, 2)
 
-    vector_grad = lax.dynamic_slice_in_dim(vector_grad, place * own, own, 1)
     found, sums = adapt(
         [
             (att_grad, planes(first_attend), planes(second_attend), planes(attend_weight)),
@@ -1216,13 +1251,15 @@
         ],
         [0, 4],
         late_sums,
-    )
-    sums = all_sum(sums, groups)
+        count if same else 0,
+    )
+    sums = lax.all_to_all(sums, AXES, 0, 0, tiled=True) if same else all_sum(sums, groups)
     adapted = [list(found[0]), *late_found, [a.T for a in found[1]]]
     *masters, trust_norms = master(
         sums,
         [found[0][2], *[a[2] for a in late_found], found[1][2]],
         [planes(attend_weight), *late_weights, vectors.T],
+        4 + cols,
     )
     masters[4] = masters[4].T
     adapted[0] = [planes(a) for a in adapted[0]]

time: 404 us -> 393 us (0.973)
  blocking collectives: 0 us -> 11.8 us
  starting transfers between devices: 50.4 us -> 38.9 us
  waiting for transfers between devices: 76.2 us -> 66.1 us
    ppermute x48 -> x34, starting transfers between devices: 50.4 us -> 34.9 us  [swap(): return lax.ppermute(value, AXES, [(i, i ^ mask) for i in range(count)])]
    ppermute x48 -> x34, waiting for transfers between devices: 63.3 us -> 49.9 us  [swap(): return lax.ppermute(value, AXES, [(i, i ^ mask) for i in range(count)])]
    all_to_all x0 -> x1, blocking collectives: none -> 11.8 us  [shards(): lax.all_to_all(sums, AXES, 0, 0, tiled=True)]
    all_to_all x0 -> x1, waiting for transfers between devices: none -> 5.74 us  [shards(): vector_grad = lax.all_to_all(sum_parts, AXES, 0, 0, tiled=True)]
  transfers between devices with their start and end apart: 49 -> 36, of which waited for: 21 -> 9; matrix products, arithmetic and copies ran while one was open for 5% -> 5% of each run, Pallas kernels for 37% -> 39%
where the time goes in v2:
time: 393 us; the launch traced here: 390 us
  Pallas kernels  215 us (55%)
  waiting for transfers between devices  66.1 us (17%)
  starting transfers between devices  38.9 us (10%)
  other arithmetic  31.8 us (8%)
  between operations  14.9 us (4%)
  blocking collectives  11.8 us (3%)
  local copies, waits for them, and re-layouts  11.2 us (3%)
    ppermute x34, waiting for transfers between devices, swap(): return lax.ppermute(value, AXES, [(i, i ^ mask) for i in range(count)])  49.9 us
    pallas_call x1, Pallas kernels, mlp_forward(): pl.pallas_call(mlp_forward_kernel, grid=(tokens // tile,), in_specs=Late....  39.9 us
    pallas_call x1, Pallas kernels, mlp_backward(): pl.pallas_call(mlp_backward_kernel, grid=(tokens // tile,), in_specs=Late...  36.1 us
    ppermute x34, starting transfers between devices, swap(): return lax.ppermute(value, AXES, [(i, i ^ mask) for i in range(count)])  34.9 us
    pallas_call x2, Pallas kernels, attend_backward(): pl.pallas_call(attend_backward_kernel, grid=(high - low,), in_specs=in_sp...  27.8 us
    pallas_call x1, Pallas kernels, attend_forward(): pl.pallas_call(kernel, grid=(rows * pairs,), in_specs=[start_spec] + qkv_...  20.2 us
    pallas_call x1, Pallas kernels, mid_weight_grad(): pl.pallas_call(mid_weight_grad_kernel, grid=(5,), in_specs=[SCALARS, whol...  20 us
    pallas_call x1, Pallas kernels, reduce_weight_grad(): pl.pallas_call(reduce_weight_grad_kernel, grid=(hidden // model,), in_spe...  16.8 us
  transfers between devices with their start and end apart: 36, of which 9 were waited for; matrix products, arithmetic and copies ran while one was open for 5% of the time, Pallas kernels for 39%

profile of v2, /device:TPU:0, one launch (start us, length us, event | category | flops | bytes accessed | tf_op | source)
XLA Modules:
  0.0 389.6 jit_solution(17835684953621437048)
XLA Ops:
  12.2 2.7 collective-permute-start.1
  14.9 2.6 collective-permute-start.2
  17.5 4.4 %collective-permute-done.1 = bf16[1,112,576]{2,1,0:T(8,128)(2,1)S(1)} collective-permute-done((bf16[1,112,576]{2,1,0:T(8,128)(2,1)S(1)}, bf16[1,112,576]{2,1,0:T(8,128)(2,1)S(1)}, u32[]{:S(2)}, u32[]{:S(2)}) %collective-permute-start.1) | collective-permute-done | bytes 129056 | tf_op jit(solution)/shard_map/ppermute | solution.py:759
  21.9 8.6 %collective-permute-done.2 = bf16[1,112,576]{2,1,0:T(8,128)(2,1)S(1)} collective-permute-done((bf16[1,112,576]{2,1,0:T(8,128)(2,1)S(1)}, bf16[1,112,576]{2,1,0:T(8,128)(2,1)S(1)}, u32[]{:S(2)}, u32[]{:S(2)}) %collective-permute-start.2) | collective-permute-done | bytes 129056 | tf_op jit(solution)/shard_map/ppermute | solution.py:759
  34.4 11.3 %collective-permute-done.4 = bf16[4,112,576]{2,1,0:T(8,128)(2,1)S(1)} collective-permute-done((bf16[4,112,576]{2,1,0:T(8,128)(2,1)S(1)}, bf16[4,112,576]{2,1,0:T(8,128)(2,1)S(1)}, u32[]{:S(2)}, u32[]{:S(2)}) %collective-permute-start.4) | collective-permute-done | bytes 516128 | tf_op jit(solution)/shard_map/ppermute | solution.py:759
  45.8 4.6 %collective-permute-done.5 = bf16[4,112,576]{2,1,0:T(8,128)(2,1)S(1)} collective-permute-done((bf16[4,112,576]{2,1,0:T(8,128)(2,1)S(1)}, bf16[4,112,576]{2,1,0:T(8,128)(2,1)S(1)}, u32[]{:S(2)}, u32[]{:S(2)}) %collective-permute-start.5) | collective-permute-done | bytes 516128 | tf_op jit(solution)/shard_map/ppermute | solution.py:759
  50.5 15.2 %collective-permute-done.6 = bf16[4,112,576]{2,1,0:T(8,128)(2,1)S(1)} collective-permute-done((bf16[4,112,576]{2,1,0:T(8,128)(2,1)S(1)}, bf16[4,112,576]{2,1,0:T(8,128)(2,1)S(1)}, u32[]{:S(2)}, u32[]{:S(2)}) %collective-permute-start.6) | collective-permute-done | bytes 516128 | tf_op jit(solution)/shard_map/ppermute | solution.py:759
  70.5 15.0 %project.1 = (bf16[2048,768]{1,0:T(8,128)(2,1)}, bf16[2048,2304]{1,0:T(8,128)(2,1)}, bf16[768,2304]{1,0:T(8,128)(2,1)}, f32[12,768]{1,0:T(8,128)}) custom-call(s32[1]{0:T(128)} %bitcast.5.refs_0_.place_ref, bf16[2048,768]{1,0:T(8,128)(2,1)} %bitcast.118, bf16[16,112,576]{2,1,0:T(8,128)(2,1)} %copy-done.18, bf16[16,112,576]{2,1,0:T(8,128)(2,1)} %collective-permute-done.7.refs_3_), custom_call_target="tpu_custom_call" | custom-call | flops 4060000000 | bytes 262144 | tf_op jit(solution)/shard_map/project/pallas_call | solution.py:312
  85.5 20.2 %attend_forward.1 = (bf16[2048,768]{1,0:T(8,128)(2,1)}, bf16[2,6,8,384,256]{4,3,2,1,0:T(8,128)(2,1)}) custom-call(s32[2,1,1024]{2,1,0:T(1,128)} %reshape.250.refs_0_, bf16[2048,2304]{1,0:T(8,128)(2,1)} %get-tuple-element.135.refs_1_.refs_2_.refs_3_.q_ref.k_ref.v_ref, bf16[2048,2304]{1,0:T(8,128)(2,1)} %get-tuple-element.135.refs_1_.refs_2_.refs_3_.q_ref.k_ref.v_ref, ...), custom_call_target="tpu_custom_call" | custom-call | flops 5219999744 | bytes 262144 | tf_op jit(solution)/shard_map/attend_forward/pallas_call | solution.py:203
  105.6 10.4 %all-gather.3.cloned.1.call-done = bf16[7168,768]{1,0:T(8,128)(2,1)} async-done(((bf16[224,768]{1,0:T(8,128)(2,1)}), bf16[7168,768]{1,0:T(8,128)(2,1)}) %all-gather.3.cloned.1.call-update) | async-done | bytes 11010064 | tf_op jit(solution)/shard_map/all_gather | solution.py:1077
  116.1 39.9 %mlp_forward.1 = (bf16[2048,768]{1,0:T(8,128)(2,1)}, f32[2048,768]{1,0:T(8,128)}, bf16[2048,768]{1,0:T(8,128)(2,1)}, bf16[2048,3072]{1,0:T(8,128)(2,1)}, bf16[20...) custom-call(bf16[32,224,768]{2,1,0:T(8,128)(2,1)} %bitcast.137, ...), custom_call_target="tpu_custom_call" | custom-call | flops 11600000000 | bytes 262144 | tf_op jit(solution)/shard_map/mlp_forward/pallas_call | solution.py:429
  156.0 16.8 %reduce_weight_grad.1 = (bf16[16,48,768]{2,1,0:T(8,128)(2,1)}, bf16[16,48,768]{2,1,0:T(8,128)(2,1)}, bf16[16,48,768]{2,1,0:T(8,128)(2,1)}, bf16[16,48,768]{2,1,0:T(8,128)(2,1)}) custom-call(s32[1]{0:T(128)} %bitcast.5.refs_0_.place_ref, bf16[2048,3072]{1,0:T(8,128)(2,1)} %get-tuple-element.139.a_ref, bf16[2048,768]{1,0:T(8,128)(2,1)} %get-tuple-element.140.b_ref), custom_call_target="tpu_custom_call" | custom-call | flops 4350000128 | bytes 262144 | tf_op jit(solution)/shard_map/reduce_weight_grad/pallas_call | solution.py:550
  173.3 36.1 %mlp_backward.1 = (bf16[2048,3072]{1,0:T(8,128)(2,1)}, f32[2048,768]{1,0:T(8,128)}, bf16[2048,768]{1,0:T(8,128)(2,1)}, bf16[2048,768]{1,0:T(8,128)(2,1)}, f32[8,768]{1,0:T(8,128)}) custom-call(bf16[32,224,768]{2,1,0:T(8,128)(2,1)} %bitcast.138, bf16[2048,768]{1,0:T(8,128)(2,1)} %bitcast.140, f32[2048,1]{1,0:T(8,128)} %bitcast.128, ...), custom_call_target="tpu_custom_call" | custom-call | flops 10439999488 | bytes 262144 | tf_op jit(solution)/shard_map/mlp_backward/pallas_call | solution.py:487
  213.7 20.0 %mid_weight_grad.1 = (bf16[16,80,768]{2,1,0:T(8,128)(2,1)}, bf16[16,48,768]{2,1,0:T(8,128)(2,1)}, bf16[16,80,768]{2,1,0:T(8,128)(2,1)}, bf16[16,48,768]{2,1,0:T(8,128)(2,1)}) custom-call(s32[1]{0:T(128)} %bitcast.5.refs_0_.place_ref, bf16[2048,768]{1,0:T(8,128)(2,1)} %get-tuple-element.147.nm_ref, bf16[2048,3072]{1,0:T(8,128)(2,1)} %get-tuple-element.158.gpre_ref, ...), custom_call_target="tpu_custom_call" | custom-call | flops 5510000128 | bytes 262144 | tf_op jit(solution)/shard_map/mid_weight_grad/pallas_call | solution.py:621
  240.3 8.3 %attend_backward.2.rest_0_ = bf16[3,2048,768]{2,1,0:T(8,128)(2,1)} custom-call(bf16[2048,2304]{1,0:T(8,128)(2,1)} %get-tuple-element.135.refs_1_.refs_2_.refs_3_.q_ref.k_ref.v_ref, bf16[2048,2304]{1,0:T(8,128)(2,1)} %get-tuple-element.135.refs_1_.refs_2_.refs_3_.q_ref.k_ref.v_ref, ...), custom_call_target="tpu_custom_call" | custom-call | flops 1740000000 | bytes 262144 | tf_op jit(solution)/shard_map/attend_backward/pallas_call | solution.py:230
  251.3 2.3 add_bitcast_fusion.1
  255.6 2.0 add_convert_fusion.1
  263.1 2.1 collective-permute-start.20
  265.2 19.5 %attend_backward.3.refs_2_.d_ref = bf16[3,2048,768]{2,1,0:T(8,128)(2,1)} custom-call(bf16[2048,2304]{1,0:T(8,128)(2,1)} %get-tuple-element.135.refs_1_.refs_2_.refs_3_.q_ref.k_ref.v_ref, bf16[2048,2304]{1,0:T(8,128)(2,1)} %get-tuple-element.135.refs_1_.refs_2_.refs_3_.q_ref.k_ref.v_ref, ...), custom_call_target="tpu_custom_call", output_to_operand_aliasing={{}: (6, {})} | custom-call | flops 5219999744 | bytes 262144 | tf_op jit(solution)/shard_map/attend_backward/pallas_call | solution.py:230
  286.7 2.0 add_convert_fusion.7
  290.7 13.8 %attend_weight_grad.1 = (bf16[16,96,576]{2,1,0:T(8,128)(2,1)}, bf16[16,96,576]{2,1,0:T(8,128)(2,1)}) custom-call(s32[1]{0:T(128)} %bitcast.5.refs_0_.place_ref, bf16[2048,768]{1,0:T(8,128)(2,1)} %get-tuple-element.192.refs_1_, bf16[3,2048,768]{2,1,0:T(8,128)(2,1)} %attend_backward.3.refs_2_.d_ref), custom_call_target="tpu_custom_call" | custom-call | flops 3769999872 | bytes 262144 | tf_op jit(solution)/shard_map/attend_weight_grad/pallas_call | solution.py:671
  304.5 2.1 add_bitcast_fusion.3
  306.7 2.3 add_bitcast_fusion
  318.0 4.1 %collective-permute-done.27 = bf16[128,768]{1,0:T(8,128)(2,1)S(1)} collective-permute-done((bf16[128,768]{1,0:T(8,128)(2,1)S(1)}, bf16[128,768]{1,0:T(8,128)(2,1)S(1)}, u32[]{:S(2)}, u32[]{:S(2)}) %collective-permute-start.27) | collective-permute-done | bytes 196640 | tf_op jit(solution)/shard_map/ppermute | solution.py:759
  323.6 16.7 %input_grad.1 = (bf16[2048,768]{1,0:T(8,128)(2,1)}, f32[12,768]{1,0:T(8,128)}, f32[32,16,128]{2,1,0:T(8,128)}) custom-call(bf16[3,2048,768]{2,1,0:T(8,128)(2,1)} %attend_backward.3.refs_2_.d_ref, bf16[2048,768]{1,0:T(8,128)(2,1)} %bitcast.120, f32[2048,768]{1,0:T(8,128)} %get-tuple-element.204.gm_ref, bf16[768,2304]{1,0:T(8,128)(2,1)} %get-tuple-element.205.w_ref, ...), custom_call_target="tpu_custom_call" | custom-call | flops 4640000000 | bytes 262144 | tf_op jit(solution)/shard_map/input_grad/pallas_call | solution.py:713
  343.8 2.9 collective-permute-start.32
  348.2 4.0 %all-to-all-start = ((f32[32,16,128]{2,1,0:T(8,128)}), f32[32,16,128]{2,1,0:T(8,128)S(1)}, u32[]{:S(2)}, u32[]{:S(2)}) async-start(f32[32,16,128]{2,1,0:T(8,128)} %get-tuple-element.228), calls=%async_computation | async-start | bytes 524288 | tf_op jit(solution)/shard_map/all_to_all | solution.py:1226
  353.7 3.5 adapt.2
  359.0 5.7 %all-to-all-done.refs_4_ = f32[32,16,128]{2,1,0:T(8,128)S(1)} async-done(((f32[32,16,128]{2,1,0:T(8,128)}), f32[32,16,128]{2,1,0:T(8,128)S(1)}, u32[]{:S(2)}, u32[]{:S(2)}) %all-to-all-start) | async-done | bytes 262176 | tf_op jit(solution)/shard_map/all_to_all | solution.py:1226
  365.4 2.6 adapt.3
  368.0 11.8 %all_to_all.10.sum_ref = f32[32,8,128]{2,1,0:T(8,128)} all-to-all(f32[32,8,128]{2,1,0:T(8,128)} %get-tuple-element.240), channel_id=1, replica_groups=mesh['batch'=8,'head'=4] {'batch','head'}, dimensions={0} | all-to-all | bytes 262144 | tf_op jit(solution)/shard_map/all_to_all | solution.py:1256
  379.9 2.6 master.1
  (161 shorter events, 58.4 us)
Async XLA Ops:
  7.2 108.9 %all-gather.3.cloned.1.call-start = ((), (), s32[]{:S(2)}) async-start(), calls=%async_computation.2 | async-start | bytes 11354112 | tf_op jit(solution)/shard_map/all_gather | solution.py:1077
  12.2 9.7 %collective-permute-start.1 = (bf16[1,112,576]{2,1,0:T(8,128)(2,1)S(1)}, bf16[1,112,576]{2,1,0:T(8,128)(2,1)S(1)}, u32[]{:S(2)}, u32[]{:S(2)}) collective-permute-start(bf16[1,112,576]{2,1,0:T(8,128)(2,1)S(1)} %fusion.9), channel_id=1, source_target_pairs={{0,8},{1,9},{2,10},{3,11},{4,12},{5,13},{6,14},{7,15},{8,0},{9,1},... | collective-permute-start | bytes 387080 | tf_op jit(solution)/shard_map/ppermute | solution.py:759
  14.9 15.7 %collective-permute-start.2 = (bf16[1,112,576]{2,1,0:T(8,128)(2,1)S(1)}, bf16[1,112,576]{2,1,0:T(8,128)(2,1)S(1)}, u32[]{:S(2)}, u32[]{:S(2)}) collective-permute-start(bf16[1,112,576]{2,1,0:T(8,128)(2,1)S(1)} %fusion.9), channel_id=1, source_target_pairs={{0,16},{1,17},{2,18},{3,19},{4,20},{5,21},{6,22},{7,23},{8,24},{9,... | collective-permute-start | bytes 387080 | tf_op jit(solution)/shard_map/ppermute | solution.py:759
  17.5 13.1 %collective-permute-start.3 = (bf16[1,112,576]{2,1,0:T(8,128)(2,1)S(1)}, bf16[1,112,576]{2,1,0:T(8,128)(2,1)S(1)}, u32[]{:S(2)}, u32[]{:S(2)}) collective-permute-start(bf16[1,112,576]{2,1,0:T(8,128)(2,1)S(1)} %fusion.9), channel_id=1, source_target_pairs={{0,24},{1,25},{2,26},{3,27},{4,28},{5,29},{6,30},{7,31},{8,16},{9,... | collective-permute-start | bytes 387080 | tf_op jit(solution)/shard_map/ppermute | solution.py:759
  30.7 15.1 %collective-permute-start.4 = (bf16[4,112,576]{2,1,0:T(8,128)(2,1)S(1)}, bf16[4,112,576]{2,1,0:T(8,128)(2,1)S(1)}, u32[]{:S(2)}, u32[]{:S(2)}) collective-permute-start(bf16[4,112,576]{2,1,0:T(8,128)(2,1)S(1)} %pad_maximum_fusion), channel_id=1, source_target_pairs={{0,2},{1,3},{2,0},{3,1},{4,6},{5,7},{6,4},{7,5},{8,10},{9,11},{10,... | collective-permute-start | bytes 1548296 | tf_op jit(solution)/shard_map/ppermute | solution.py:759
  32.2 18.2 %collective-permute-start.5 = (bf16[4,112,576]{2,1,0:T(8,128)(2,1)S(1)}, bf16[4,112,576]{2,1,0:T(8,128)(2,1)S(1)}, u32[]{:S(2)}, u32[]{:S(2)}) collective-permute-start(bf16[4,112,576]{2,1,0:T(8,128)(2,1)S(1)} %pad_maximum_fusion), channel_id=1, source_target_pairs={{0,4},{1,5},{2,6},{3,7},{4,0},{5,1},{6,2},{7,3},{8,12},{9,13},{10,... | collective-permute-start | bytes 1548296 | tf_op jit(solution)/shard_map/ppermute | solution.py:759
  33.9 31.8 %collective-permute-start.6 = (bf16[4,112,576]{2,1,0:T(8,128)(2,1)S(1)}, bf16[4,112,576]{2,1,0:T(8,128)(2,1)S(1)}, u32[]{:S(2)}, u32[]{:S(2)}) collective-permute-start(bf16[4,112,576]{2,1,0:T(8,128)(2,1)S(1)} %pad_maximum_fusion), channel_id=1, source_target_pairs={{0,6},{1,7},{2,4},{3,5},{4,2},{5,3},{6,0},{7,1},{8,14},{9,15},{10,... | collective-permute-start | bytes 1548296 | tf_op jit(solution)/shard_map/ppermute | solution.py:759
  172.8 36.6 %collective-permute-start.8 = (bf16[16,48,768]{2,1,0:T(8,128)(2,1)}, bf16[16,48,768]{2,1,0:T(8,128)(2,1)S(1)}, u32[]{:S(2)}, u32[]{:S(2)}) collective-permute-start(bf16[16,48,768]{2,1,0:T(8,128)(2,1)} %get-tuple-element.150), channel_id=1, source_target_pairs={{0,1},{1,0},{2,3},{3,2},{4,5},{5,4},{6,7},{7,6},{8,9},{9,8},{10,11... | collective-permute-start | bytes 3538952 | tf_op jit(solution)/shard_map/ppermute | solution.py:759
  173.0 36.4 %collective-permute-start.9 = (bf16[16,48,768]{2,1,0:T(8,128)(2,1)}, bf16[16,48,768]{2,1,0:T(8,128)(2,1)S(1)}, u32[]{:S(2)}, u32[]{:S(2)}) collective-permute-start(bf16[16,48,768]{2,1,0:T(8,128)(2,1)} %get-tuple-element.152), channel_id=1, source_target_pairs={{0,1},{1,0},{2,3},{3,2},{4,5},{5,4},{6,7},{7,6},{8,9},{9,8},{10,11... | collective-permute-start | bytes 3538952 | tf_op jit(solution)/shard_map/ppermute | solution.py:759
  211.6 22.1 %collective-permute-start.10 = (bf16[8,48,768]{2,1,0:T(8,128)(2,1)S(1)}, bf16[8,48,768]{2,1,0:T(8,128)(2,1)}, u32[]{:S(2)}, u32[]{:S(2)}) collective-permute-start(bf16[8,48,768]{2,1,0:T(8,128)(2,1)S(1)} %add_convert_fusion.3), channel_id=1, source_target_pairs={{0,4},{1,5},{2,6},{3,7},{4,0},{5,1},{6,2},{7,3},{8,12},{9,13},{10,... | collective-permute-start | bytes 1769480 | tf_op jit(solution)/shard_map/ppermute | solution.py:759
  213.1 20.6 %collective-permute-start.11 = (bf16[8,48,768]{2,1,0:T(8,128)(2,1)S(1)}, bf16[8,48,768]{2,1,0:T(8,128)(2,1)S(1)}, u32[]{:S(2)}, u32[]{:S(2)}) collective-permute-start(bf16[8,48,768]{2,1,0:T(8,128)(2,1)S(1)} %add_convert_fusion.2), channel_id=1, source_target_pairs={{0,2},{1,3},{2,0},{3,1},{4,6},{5,7},{6,4},{7,5},{8,10},{9,11},{10,... | collective-permute-start | bytes 1769480 | tf_op jit(solution)/shard_map/ppermute | solution.py:759
  234.5 14.1 %collective-permute-start.12 = (bf16[16,80,768]{2,1,0:T(8,128)(2,1)}, bf16[16,80,768]{2,1,0:T(8,128)(2,1)S(1)}, u32[]{:S(2)}, u32[]{:S(2)}) collective-permute-start(bf16[16,80,768]{2,1,0:T(8,128)(2,1)} %get-tuple-element.170), channel_id=1, source_target_pairs={{0,1},{1,0},{2,3},{3,2},{4,5},{5,4},{6,7},{7,6},{8,9},{9,8},{10,11... | collective-permute-start | bytes 5898248 | tf_op jit(solution)/shard_map/ppermute | solution.py:759
  234.5 14.1 %collective-permute-start.13 = (bf16[16,48,768]{2,1,0:T(8,128)(2,1)}, bf16[16,48,768]{2,1,0:T(8,128)(2,1)S(1)}, u32[]{:S(2)}, u32[]{:S(2)}) collective-permute-start(bf16[16,48,768]{2,1,0:T(8,128)(2,1)} %get-tuple-element.172), channel_id=1, source_target_pairs={{0,1},{1,0},{2,3},{3,2},{4,5},{5,4},{6,7},{7,6},{8,9},{9,8},{10,11... | collective-permute-start | bytes 3538952 | tf_op jit(solution)/shard_map/ppermute | solution.py:759
  238.3 10.4 %collective-permute-start.14 = (bf16[4,48,768]{2,1,0:T(8,128)(2,1)}, bf16[4,48,768]{2,1,0:T(8,128)(2,1)S(1)}, u32[]{:S(2)}, u32[]{:S(2)}) collective-permute-start(bf16[4,48,768]{2,1,0:T(8,128)(2,1)} %add_convert_fusion.10), channel_id=1, source_target_pairs={{0,2},{1,3},{2,0},{3,1},{4,6},{5,7},{6,4},{7,5},{8,10},{9,11},{10,... | collective-permute-start | bytes 884744 | tf_op jit(solution)/shard_map/ppermute | solution.py:759
  239.7 8.9 %collective-permute-start.15 = (bf16[4,48,768]{2,1,0:T(8,128)(2,1)S(1)}, bf16[4,48,768]{2,1,0:T(8,128)(2,1)S(1)}, u32[]{:S(2)}, u32[]{:S(2)}) collective-permute-start(bf16[4,48,768]{2,1,0:T(8,128)(2,1)S(1)} %add_convert_fusion.9), channel_id=1, source_target_pairs={{0,4},{1,5},{2,6},{3,7},{4,0},{5,1},{6,2},{7,3},{8,12},{9,13},{10,... | collective-permute-start | bytes 884744 | tf_op jit(solution)/shard_map/ppermute | solution.py:759
  258.8 25.9 %collective-permute-start.16 = (bf16[8,80,768]{2,1,0:T(8,128)(2,1)}, bf16[8,80,768]{2,1,0:T(8,128)(2,1)}, u32[]{:S(2)}, u32[]{:S(2)}) collective-permute-start(bf16[8,80,768]{2,1,0:T(8,128)(2,1)} %add_convert_fusion), channel_id=1, source_target_pairs={{0,4},{1,5},{2,6},{3,7},{4,0},{5,1},{6,2},{7,3},{8,12},{9,13},{10,... | collective-permute-start | bytes 2949128 | tf_op jit(solution)/shard_map/ppermute | solution.py:759
  260.2 24.5 %collective-permute-start.17 = (bf16[8,48,768]{2,1,0:T(8,128)(2,1)}, bf16[8,48,768]{2,1,0:T(8,128)(2,1)}, u32[]{:S(2)}, u32[]{:S(2)}) collective-permute-start(bf16[8,48,768]{2,1,0:T(8,128)(2,1)} %add_convert_fusion.1), channel_id=1, source_target_pairs={{0,2},{1,3},{2,0},{3,1},{4,6},{5,7},{6,4},{7,5},{8,10},{9,11},{10,... | collective-permute-start | bytes 1769480 | tf_op jit(solution)/shard_map/ppermute | solution.py:759
  260.8 23.9 %collective-permute-start.18 = (bf16[96,768]{1,0:T(8,128)(2,1)}, bf16[96,768]{1,0:T(8,128)(2,1)}, u32[]{:S(2)}, u32[]{:S(2)}) collective-permute-start(bf16[96,768]{1,0:T(8,128)(2,1)} %pad_maximum_fusion.7), channel_id=1, source_target_pairs={{0,8},{1,9},{2,10},{3,11},{4,12},{5,13},{6,14},{7,15},{8,0},{9,1},... | collective-permute-start | bytes 442376 | tf_op jit(solution)/shard_map/ppermute | solution.py:759
  262.0 22.7 %collective-permute-start.19 = (bf16[96,768]{1,0:T(8,128)(2,1)}, bf16[96,768]{1,0:T(8,128)(2,1)}, u32[]{:S(2)}, u32[]{:S(2)}) collective-permute-start(bf16[96,768]{1,0:T(8,128)(2,1)} %pad_maximum_fusion.8), channel_id=1, source_target_pairs={{0,16},{1,17},{2,18},{3,19},{4,20},{5,21},{6,22},{7,23},{8,24},{9,... | collective-permute-start | bytes 442376 | tf_op jit(solution)/shard_map/ppermute | solution.py:759
  263.1 21.6 %collective-permute-start.20 = (bf16[96,768]{1,0:T(8,128)(2,1)}, bf16[96,768]{1,0:T(8,128)(2,1)}, u32[]{:S(2)}, u32[]{:S(2)}) collective-permute-start(bf16[96,768]{1,0:T(8,128)(2,1)} %pad_maximum_fusion.9), channel_id=1, source_target_pairs={{0,24},{1,25},{2,26},{3,27},{4,28},{5,29},{6,30},{7,31},{8,16},{9,... | collective-permute-start | bytes 442376 | tf_op jit(solution)/shard_map/ppermute | solution.py:759
  288.6 15.8 %collective-permute-start.21 = (bf16[4,80,768]{2,1,0:T(8,128)(2,1)}, bf16[4,80,768]{2,1,0:T(8,128)(2,1)}, u32[]{:S(2)}, u32[]{:S(2)}) collective-permute-start(bf16[4,80,768]{2,1,0:T(8,128)(2,1)} %add_convert_fusion.7), channel_id=1, source_target_pairs={{0,2},{1,3},{2,0},{3,1},{4,6},{5,7},{6,4},{7,5},{8,10},{9,11},{10,... | collective-permute-start | bytes 1474568 | tf_op jit(solution)/shard_map/ppermute | solution.py:759
  290.1 14.4 %collective-permute-start.22 = (bf16[4,48,768]{2,1,0:T(8,128)(2,1)}, bf16[4,48,768]{2,1,0:T(8,128)(2,1)}, u32[]{:S(2)}, u32[]{:S(2)}) collective-permute-start(bf16[4,48,768]{2,1,0:T(8,128)(2,1)} %add_convert_fusion.8), channel_id=1, source_target_pairs={{0,4},{1,5},{2,6},{3,7},{4,0},{5,1},{6,2},{7,3},{8,12},{9,13},{10,... | collective-permute-start | bytes 884744 | tf_op jit(solution)/shard_map/ppermute | solution.py:759
  310.4 29.9 %collective-permute-start.24 = (bf16[4,96,576]{2,1,0:T(8,128)(2,1)S(1)}, bf16[4,96,576]{2,1,0:T(8,128)(2,1)S(1)}, u32[]{:S(2)}, u32[]{:S(2)}) collective-permute-start(bf16[4,96,576]{2,1,0:T(8,128)(2,1)S(1)} %get-tuple-element.209), channel_id=1, source_target_pairs={{0,2},{1,3},{2,0},{3,1},{4,6},{5,7},{6,4},{7,5},{8,10},{9,11},{10,... | collective-permute-start | bytes 1327112 | tf_op jit(solution)/shard_map/ppermute | solution.py:759
  311.9 28.5 %collective-permute-start.25 = (bf16[4,96,576]{2,1,0:T(8,128)(2,1)S(1)}, bf16[4,96,576]{2,1,0:T(8,128)(2,1)S(1)}, u32[]{:S(2)}, u32[]{:S(2)}) collective-permute-start(bf16[4,96,576]{2,1,0:T(8,128)(2,1)S(1)} %get-tuple-element.210), channel_id=1, source_target_pairs={{0,4},{1,5},{2,6},{3,7},{4,0},{5,1},{6,2},{7,3},{8,12},{9,13},{10,... | collective-permute-start | bytes 1327112 | tf_op jit(solution)/shard_map/ppermute | solution.py:759
  312.4 27.9 %collective-permute-start.26 = (bf16[4,96,576]{2,1,0:T(8,128)(2,1)S(1)}, bf16[4,96,576]{2,1,0:T(8,128)(2,1)S(1)}, u32[]{:S(2)}, u32[]{:S(2)}) collective-permute-start(bf16[4,96,576]{2,1,0:T(8,128)(2,1)S(1)} %get-tuple-element.211), channel_id=1, source_target_pairs={{0,6},{1,7},{2,4},{3,5},{4,2},{5,3},{6,0},{7,1},{8,14},{9,15},{10,... | collective-permute-start | bytes 1327112 | tf_op jit(solution)/shard_map/ppermute | solution.py:759
  316.0 24.3 %collective-permute-start.28 = (bf16[128,768]{1,0:T(8,128)(2,1)S(1)}, bf16[128,768]{1,0:T(8,128)(2,1)}, u32[]{:S(2)}, u32[]{:S(2)}) collective-permute-start(bf16[128,768]{1,0:T(8,128)(2,1)S(1)} %pad_maximum_fusion.4), channel_id=1, source_target_pairs={{0,16},{1,17},{2,18},{3,19},{4,20},{5,21},{6,22},{7,23},{8,24},{9,... | collective-permute-start | bytes 589832 | tf_op jit(solution)/shard_map/ppermute | solution.py:759
  322.1 18.2 %collective-permute-start.29 = (bf16[128,768]{1,0:T(8,128)(2,1)S(1)}, bf16[128,768]{1,0:T(8,128)(2,1)}, u32[]{:S(2)}, u32[]{:S(2)}) collective-permute-start(bf16[128,768]{1,0:T(8,128)(2,1)S(1)} %pad_maximum_fusion.5), channel_id=1, source_target_pairs={{0,24},{1,25},{2,26},{3,27},{4,28},{5,29},{6,30},{7,31},{8,16},{9,... | collective-permute-start | bytes 589832 | tf_op jit(solution)/shard_map/ppermute | solution.py:759
  342.2 10.0 %collective-permute-start.30 = (f32[2,24,768]{2,1,0:T(8,128)S(1)}, f32[2,24,768]{2,1,0:T(8,128)S(1)}, u32[]{:S(2)}, u32[]{:S(2)}) collective-permute-start(f32[2,24,768]{2,1,0:T(8,128)S(1)} %select_bitcast_fusion.2), channel_id=1, source_target_pairs={{0,1},{1,0},{2,3},{3,2},{4,5},{5,4},{6,7},{7,6},{8,9},{9,8},{10,11... | collective-permute-start | bytes 442376 | tf_op jit(solution)/shard_map/ppermute | solution.py:759
  343.7 13.5 %collective-permute-start.31 = (bf16[96,576]{1,0:T(8,128)(2,1)S(1)}, bf16[96,576]{1,0:T(8,128)(2,1)S(1)}, u32[]{:S(2)}, u32[]{:S(2)}) collective-permute-start(bf16[96,576]{1,0:T(8,128)(2,1)S(1)} %get-tuple-element.256), channel_id=1, source_target_pairs={{0,8},{1,9},{2,10},{3,11},{4,12},{5,13},{6,14},{7,15},{8,0},{9,1},... | collective-permute-start | bytes 331784 | tf_op jit(solution)/shard_map/ppermute | solution.py:759
  343.8 13.4 %collective-permute-start.32 = (bf16[96,576]{1,0:T(8,128)(2,1)S(1)}, bf16[96,576]{1,0:T(8,128)(2,1)S(1)}, u32[]{:S(2)}, u32[]{:S(2)}) collective-permute-start(bf16[96,576]{1,0:T(8,128)(2,1)S(1)} %get-tuple-element.255), channel_id=1, source_target_pairs={{0,16},{1,17},{2,18},{3,19},{4,20},{5,21},{6,22},{7,23},{8,24},{9,... | collective-permute-start | bytes 331784 | tf_op jit(solution)/shard_map/ppermute | solution.py:759
  346.7 10.5 %collective-permute-start.33 = (bf16[96,576]{1,0:T(8,128)(2,1)S(1)}, bf16[96,576]{1,0:T(8,128)(2,1)S(1)}, u32[]{:S(2)}, u32[]{:S(2)}) collective-permute-start(bf16[96,576]{1,0:T(8,128)(2,1)S(1)} %get-tuple-element.254), channel_id=1, source_target_pairs={{0,24},{1,25},{2,26},{3,27},{4,28},{5,29},{6,30},{7,31},{8,16},{9,... | collective-permute-start | bytes 331784 | tf_op jit(solution)/shard_map/ppermute | solution.py:759
  348.2 16.6 %all-to-all-start = ((f32[32,16,128]{2,1,0:T(8,128)}), f32[32,16,128]{2,1,0:T(8,128)S(1)}, u32[]{:S(2)}, u32[]{:S(2)}) async-start(f32[32,16,128]{2,1,0:T(8,128)} %get-tuple-element.228), calls=%async_computation | async-start | bytes 524288 | tf_op jit(solution)/shard_map/all_to_all | solution.py:1226
  (25 other events, 229.2 us)
Sparse Core Ops, SparseCore 0:
  11.9 104.0 all-gather.2
